TPU v7x, 32 devices: a whole 2x2x4 slice. The times are simulated.
32 devices in a mesh: head: 2 (over x), seq: 16 (over z, y, core).
Axes of the slice: x: 2, y: 2, z: 4, core: 2. Of those that a mesh axis runs over, the one named last changes fastest.
Arguments:
- tokens: bfloat16 [12288, 3200], P('seq'), may hold values from -6 to 6
- ln_gain: float32 [3200], replicated, may hold values from 0.5 to 2
- w_query: bfloat16 [3200, 2048], P('seq', 'head')
- w_key: bfloat16 [3200, 2048], P('seq', 'head')
- w_value: bfloat16 [3200, 2048], P('seq', 'head'), may hold values from -0.109375 to 0.109375
- q_gain: float32 [2048], P('head'), may hold values from 0.5 to 8
- k_gain: float32 [2048], P('head'), may hold values from 0.5 to 8
- seg_ids: int32 [12288], P('seq'), may hold values from 0 to 22, never falling along the last dimension, each value on 1 to 1025 neighbouring positions
Outputs:
- attended: bfloat16 [12288, 2048], P('seq', 'head')
Inputs may be any that keep to these rules, and one draw needn't show every extreme that they name: `seg_ids`: ids never fall along the tokens; each id covers 1 to 1025 consecutive tokens and one covers exactly 1025.
All inputs are finite; a program needn't handle non-finite values.
Results may differ from a plain program's by a relative error of at most 0.0055.
The roundings to bfloat16 on the way count: a program that leaves them out, or rounds other values in their place, can miss the bound.
Values may be sent and summed in bfloat16 or wider, within the bound.
A program may use at most 192 MiB of HBM per device.

v0:
```python
import math

import jax
import jax.numpy as jnp
from jax import lax
from jax.sharding import PartitionSpec as P

HEADS = 16
HEAD_DIM = 128
MOST = 1025


EPS = 1e-06


def from_behind(shard, axis, by):
    size = lax.axis_size(axis)
    pairs = [(i, i + by) for i in range(size) if 0 <= i + by < size]
    return lax.ppermute(shard, axis, pairs)


def on_device(tokens, ln_gain, w_query, w_key, w_value, q_gain, k_gain, seg_ids):
    rows_here = tokens.shape[0]
    channels = w_query.shape[1]
    heads_here = channels // HEAD_DIM
    total_channels = HEADS * HEAD_DIM
    floats = tokens.astype(jnp.float32)
    normed = (
        floats * lax.rsqrt(jnp.mean(floats * floats, axis=1, keepdims=True) + EPS) * ln_gain
    ).astype(jnp.bfloat16)

    def add_rows(block_rows):
        return jnp.dot(normed, block_rows, preferred_element_type=jnp.float32)

    queries = add_rows(lax.all_gather(w_query, "seq", axis=0, tiled=True))
    key_part = add_rows(lax.all_gather(w_key, "seq", axis=0, tiled=True))
    value_part = add_rows(lax.all_gather(w_value, "seq", axis=0, tiled=True))
    square_q, square_k = lax.psum(
        (jnp.sum(queries * queries, axis=1), jnp.sum(key_part * key_part, axis=1)), "head"
    )
    q_hat = (queries * lax.rsqrt(square_q[:, None] / total_channels + EPS) * q_gain).astype(
        jnp.bfloat16
    )
    k_hat = (key_part * lax.rsqrt(square_k[:, None] / total_channels + EPS) * k_gain).astype(
        jnp.bfloat16
    )
    v_hat = value_part.astype(jnp.bfloat16)
    packed = jnp.concatenate([k_hat, v_hat], axis=1)
    marks = (seg_ids + 1).astype(jnp.bfloat16)
    reach = (MOST + rows_here - 2) // rows_here
    left_side = []
    right_side = []
    for distance in range(1, reach + 1):
        for direction in (1, -1):
            arrived = from_behind((packed, marks), "seq", direction * distance)
            if direction > 0:
                left_side.insert(0, arrived)
            else:
                right_side.append(arrived)
    window = left_side + [(packed, marks)] + right_side
    near_keys = jnp.concatenate([entry[0] for entry in window], axis=0)
    near_marks = jnp.concatenate([entry[1] for entry in window], axis=0)
    allowed = marks[:, None] == near_marks[None, :]
    scale = 1.0 / math.sqrt(HEAD_DIM)
    outputs = []
    for head_index in range(heads_here):
        first_col = head_index * HEAD_DIM
        q_head = q_hat[:, first_col : first_col + HEAD_DIM]
        k_head = near_keys[:, first_col : first_col + HEAD_DIM]
        v_head = near_keys[:, channels + first_col : channels + first_col + HEAD_DIM]
        scores = jnp.einsum("qd,kd->qk", q_head, k_head, preferred_element_type=jnp.float32) * scale
        scores = jnp.where(allowed, scores, -1e30)
        highest = jnp.max(scores, axis=1, keepdims=True)
        expo = jnp.exp(scores - highest)
        weights = (expo / jnp.sum(expo, axis=1, keepdims=True)).astype(jnp.bfloat16)
        outputs.append(
            jnp.dot(weights, v_head, preferred_element_type=jnp.float32).astype(jnp.bfloat16)
        )
    return jnp.concatenate(outputs, axis=1)


def solution(mesh):
    return jax.shard_map(
        on_device,
        mesh=mesh,
        in_specs=(
            P("seq", None),
            P(),
            P("seq", "head"),
            P("seq", "head"),
            P("seq", "head"),
            P("head"),
            P("head"),
            P("seq"),
        ),
        out_specs=P("seq", "head"),
        check_vma=False,
    )
```

profile of v0, /device:TPU:0, one launch (start us, length us, event | category | flops | bytes accessed | tf_op | source)
XLA Modules:
  0.0 595.5 jit_solution(5773370806372243804)
XLA Ops:
  12.2 63.6 %all-gather.6.cloned.1.call-done = bf16[3200,1024]{1,0:T(8,128)(2,1)} async-done(((bf16[200,1024]{1,0:T(8,128)(2,1)}), bf16[3200,1024]{1,0:T(8,128)(2,1)}) %all-gather.6.cloned.1.call-update) | async-done | bytes 6553616 | tf_op jit(solution)/shard_map/all_gather | solution.py:36
  75.8 10.7 %multiply_reduce_fusion = (f32[768]{0:T(1024)S(1)}, f32[768,1024]{1,0:T(8,128)}) fusion(bf16[3200,1024]{1,0:T(8,128)(2,1)} %all-gather.6.cloned.1.call-done, bf16[768,3200]{1,0:T(8,128)(2,1)} %param.8, f32[3200]{0:T(1024)} %param.9, f32[768]{0:T(1024)S(1)} %add_rsqrt_fusion.2), kind=kOutput, calls=%fused_computation.47 | convolution fusion | flops 5044567040 | bytes 14633472 | tf_op jit(solution)/shard_map/dot_general | solution.py:33
  86.5 53.4 %all-gather.4.cloned.1.call-done = bf16[3200,1024]{1,0:T(8,128)(2,1)} async-done(((bf16[200,1024]{1,0:T(8,128)(2,1)}), bf16[3200,1024]{1,0:T(8,128)(2,1)}) %all-gather.4.cloned.1.call-update) | async-done | bytes 6553616 | tf_op jit(solution)/shard_map/all_gather | solution.py:35
  140.0 10.7 %multiply_reduce_fusion.1 = (f32[768]{0:T(1024)S(1)}, f32[768,1024]{1,0:T(8,128)}) fusion(bf16[3200,1024]{1,0:T(8,128)(2,1)} %all-gather.4.cloned.1.call-done, bf16[768,3200]{1,0:T(8,128)(2,1)} %param.8, f32[3200]{0:T(1024)S(1)} %copy-done.4, f32[768]{0:T(1024)S(1)} %add_rsqrt_fusion.2), kind=kOutput, calls=%fused_computation.49 | convolution fusion | flops 5044567040 | bytes 14633472 | tf_op jit(solution)/shard_map/dot_general | solution.py:33
  150.7 5.0 all-reduce
  157.9 46.3 %all-gather.8.cloned.1.call-done = bf16[3200,1024]{1,0:T(8,128)(2,1)} async-done(((bf16[200,1024]{1,0:T(8,128)(2,1)}), bf16[3200,1024]{1,0:T(8,128)(2,1)}) %all-gather.8.cloned.1.call-update) | async-done | bytes 6553616 | tf_op jit(solution)/shard_map/all_gather | solution.py:37
  204.2 9.4 %convolution_convert_fusion = bf16[768,1024]{1,0:T(8,128)(2,1)S(1)} fusion(bf16[3200,1024]{1,0:T(8,128)(2,1)} %all-gather.8.cloned.1.call-done, bf16[768,3200]{1,0:T(8,128)(2,1)} %param.8, f32[3200]{0:T(1024)S(1)} %copy-done.4, f32[768]{0:T(1024)S(1)} %add_rsqrt_fusion.2), kind=kOutput, calls=%fused_computation.50 | convolution fusion | flops 5043781632 | bytes 13057536 | tf_op jit(solution)/shard_map/dot_general | solution.py:33
  215.7 4.1 collective-permute-start.4
  225.9 4.5 collective-permute-start
  230.5 157.5 %collective-permute-done = bf16[768]{0:T(1024)(128)(2,1)S(1)} collective-permute-done((bf16[768]{0:T(1024)(128)(2,1)S(1)}, bf16[768]{0:T(1024)(128)(2,1)S(1)}, u32[]{:S(2)}, u32[]{:S(2)}) %collective-permute-start) | collective-permute-done | bytes 1568 | tf_op jit(solution)/shard_map/ppermute | solution.py:19
  388.0 35.1 %collective-permute-start.1 = (bf16[768]{0:T(1024)(128)(2,1)S(1)}, bf16[768]{0:T(1024)(128)(2,1)S(1)}, u32[]{:S(2)}, u32[]{:S(2)}) collective-permute-start(bf16[768]{0:T(1024)(128)(2,1)S(1)} %add_convert_fusion), channel_id=1, source_target_pairs={{0,1},{1,2},{2,3},{3,4},{4,5},{5,6},{6,7},{7,8},{8,9},{9,10},{10,1... | collective-permute-start | bytes 4616 | tf_op jit(solution)/shard_map/ppermute | solution.py:19
  444.6 6.2 %fusion.64 = (f32[768]{0:T(1024)S(1)}, f32[768,3840]{1,0:T(8,128)}) fusion(bf16[3840,2048]{1,0:T(8,128)(2,1)S(1)} %constant_dynamic-update-slice_fusion, bf16[768,1024]{1,0:T(8,128)(2,1)S(1)} %multiply_convert_fusion.1, bf16[3840]{0:T(1024)(128)(2,1)S(1)} %constant_dynamic-update-slice_fusion.5, bf16[768]{0:T(1024)(128)(2,1)S(1)} %add_convert_fusion), kind=kOutput, calls=%fused_computation.103 | convolution fusion | flops 766770432 | bytes 12989440 | tf_op jit(solution)/shard_map/qd,kd->qk/dot_general | solution.py:71
  450.8 6.4 %fusion.65 = (f32[768]{0:T(1024)S(1)}, f32[768,3840]{1,0:T(8,128)}) fusion(bf16[3840,2048]{1,0:T(8,128)(2,1)S(1)} %constant_dynamic-update-slice_fusion, bf16[768,1024]{1,0:T(8,128)(2,1)S(1)} %multiply_convert_fusion.1, bf16[3840]{0:T(1024)(128)(2,1)S(1)} %constant_dynamic-update-slice_fusion.5, bf16[768]{0:T(1024)(128)(2,1)S(1)} %add_convert_fusion), kind=kOutput, calls=%fused_computation.104 | convolution fusion | flops 766770432 | bytes 12989440 | tf_op jit(solution)/shard_map/qd,kd->qk/dot_general | solution.py:71
  457.2 5.5 fusion.66
  462.7 5.5 fusion.67
  468.2 5.5 fusion.68
  473.8 5.7 fusion.69
  479.4 5.8 fusion.70
  488.5 6.0 %fusion = f32[768]{0:T(1024)S(1)} fusion(f32[768,3840]{1,0:T(8,128)} %get-tuple-element.12, f32[768]{0:T(1024)S(1)} %get-tuple-element.11), kind=kLoop, calls=%fused_computation.26 | loop fusion | flops 5897472 | bytes 11802624 | tf_op jit(solution)/shard_map/reduce_sum | solution.py:75
  494.6 7.2 %fusion.27 = bf16[768,1024]{0,1:T(8,128)(2,1)S(1)} fusion(f32[768,3840]{1,0:T(8,128)} %get-tuple-element.12, f32[768]{0:T(1024)S(1)} %fusion, f32[768]{0:T(1024)S(1)} %get-tuple-element.11, bf16[3840,2048]{1,0:T(8,128)(2,1)} %copy-done), kind=kOutput, calls=%fused_computation.59 | convolution fusion | flops 763920384 | bytes 12982272 | tf_op jit(solution)/shard_map/dot_general | solution.py:77
  501.8 6.0 %fusion.1 = f32[768]{0:T(1024)S(1)} fusion(f32[768,3840]{1,0:T(8,128)} %get-tuple-element.14, f32[768]{0:T(1024)S(1)} %get-tuple-element.13), kind=kLoop, calls=%fused_computation.27 | loop fusion | flops 5897472 | bytes 11802624 | tf_op jit(solution)/shard_map/reduce_sum | solution.py:75
  507.8 7.1 %fusion.28 = bf16[768,1024]{0,1:T(8,128)(2,1)S(1)} fusion(bf16[768,1024]{0,1:T(8,128)(2,1)S(1)} %fusion.27, f32[768,3840]{1,0:T(8,128)} %get-tuple-element.14, f32[768]{0:T(1024)S(1)} %fusion.1, f32[768]{0:T(1024)S(1)} %get-tuple-element.13, bf16[3840,2048]{1,0:T(8,128)(2,1)} %copy-done), kind=kOutput, calls=%fused_computation.60 | convolution fusion | flops 763920384 | bytes 12984320 | tf_op jit(solution)/shard_map/dot_general | solution.py:77
  515.0 6.0 %fusion.2 = f32[768]{0:T(1024)S(1)} fusion(f32[768,3840]{1,0:T(8,128)} %get-tuple-element.16, f32[768]{0:T(1024)S(1)} %get-tuple-element.15), kind=kLoop, calls=%fused_computation.28 | loop fusion | flops 5897472 | bytes 11802624 | tf_op jit(solution)/shard_map/reduce_sum | solution.py:75
  521.0 7.3 %fusion.29 = bf16[768,1024]{0,1:T(8,128)(2,1)S(1)} fusion(bf16[768,1024]{0,1:T(8,128)(2,1)S(1)} %fusion.28, f32[768,3840]{1,0:T(8,128)} %get-tuple-element.16, f32[768]{0:T(1024)S(1)} %fusion.2, f32[768]{0:T(1024)S(1)} %get-tuple-element.15, bf16[3840,2048]{1,0:T(8,128)(2,1)} %copy-done), kind=kOutput, calls=%fused_computation.61 | convolution fusion | flops 763920384 | bytes 12984320 | tf_op jit(solution)/shard_map/dot_general | solution.py:77
  528.3 6.0 %fusion.3 = f32[768]{0:T(1024)S(1)} fusion(f32[768,3840]{1,0:T(8,128)} %get-tuple-element.18, f32[768]{0:T(1024)S(1)} %get-tuple-element.17), kind=kLoop, calls=%fused_computation.29 | loop fusion | flops 5897472 | bytes 11802624 | tf_op jit(solution)/shard_map/reduce_sum | solution.py:75
  534.4 7.1 %fusion.30 = bf16[768,1024]{0,1:T(8,128)(2,1)S(1)} fusion(bf16[768,1024]{0,1:T(8,128)(2,1)S(1)} %fusion.29, f32[768,3840]{1,0:T(8,128)} %get-tuple-element.18, f32[768]{0:T(1024)S(1)} %fusion.3, f32[768]{0:T(1024)S(1)} %get-tuple-element.17, bf16[3840,2048]{1,0:T(8,128)(2,1)} %copy-done), kind=kOutput, calls=%fused_computation.62 | convolution fusion | flops 763920384 | bytes 12984320 | tf_op jit(solution)/shard_map/dot_general | solution.py:77
  541.5 6.0 %fusion.4 = f32[768]{0:T(1024)S(1)} fusion(f32[768,3840]{1,0:T(8,128)} %get-tuple-element.20, f32[768]{0:T(1024)S(1)} %get-tuple-element.19), kind=kLoop, calls=%fused_computation.30 | loop fusion | flops 5897472 | bytes 11802624 | tf_op jit(solution)/shard_map/reduce_sum | solution.py:75
  547.5 7.1 %fusion.31 = bf16[768,1024]{0,1:T(8,128)(2,1)S(1)} fusion(bf16[768,1024]{0,1:T(8,128)(2,1)S(1)} %fusion.30, f32[768,3840]{1,0:T(8,128)} %get-tuple-element.20, f32[768]{0:T(1024)S(1)} %fusion.4, f32[768]{0:T(1024)S(1)} %get-tuple-element.19, bf16[3840,2048]{1,0:T(8,128)(2,1)} %copy-done), kind=kOutput, calls=%fused_computation.63 | convolution fusion | flops 763920384 | bytes 12984320 | tf_op jit(solution)/shard_map/dot_general | solution.py:77
  554.6 6.0 %fusion.5 = f32[768]{0:T(1024)S(1)} fusion(f32[768,3840]{1,0:T(8,128)} %get-tuple-element.22, f32[768]{0:T(1024)S(1)} %get-tuple-element.21), kind=kLoop, calls=%fused_computation.31 | loop fusion | flops 5897472 | bytes 11802624 | tf_op jit(solution)/shard_map/reduce_sum | solution.py:75
  560.7 7.4 %fusion.32 = bf16[768,1024]{0,1:T(8,128)(2,1)S(1)} fusion(bf16[768,1024]{0,1:T(8,128)(2,1)S(1)} %fusion.31, f32[768,3840]{1,0:T(8,128)} %get-tuple-element.22, f32[768]{0:T(1024)S(1)} %fusion.5, f32[768]{0:T(1024)S(1)} %get-tuple-element.21, bf16[3840,2048]{1,0:T(8,128)(2,1)} %copy-done), kind=kOutput, calls=%fused_computation.64 | convolution fusion | flops 763920384 | bytes 12984320 | tf_op jit(solution)/shard_map/dot_general | solution.py:77
  568.1 6.0 %fusion.6 = f32[768]{0:T(1024)S(1)} fusion(f32[768,3840]{1,0:T(8,128)} %get-tuple-element.24, f32[768]{0:T(1024)S(1)} %get-tuple-element.23), kind=kLoop, calls=%fused_computation.32 | loop fusion | flops 5897472 | bytes 11802624 | tf_op jit(solution)/shard_map/reduce_sum | solution.py:75
  574.1 7.1 %fusion.33 = bf16[768,1024]{0,1:T(8,128)(2,1)S(1)} fusion(bf16[768,1024]{0,1:T(8,128)(2,1)S(1)} %fusion.32, f32[768,3840]{1,0:T(8,128)} %get-tuple-element.24, f32[768]{0:T(1024)S(1)} %fusion.6, f32[768]{0:T(1024)S(1)} %get-tuple-element.23, bf16[3840,2048]{1,0:T(8,128)(2,1)} %copy-done), kind=kOutput, calls=%fused_computation.65 | convolution fusion | flops 763920384 | bytes 12984320 | tf_op jit(solution)/shard_map/dot_general | solution.py:77
  (51 shorter events, 48.1 us)
Async XLA Ops:
  6.5 69.2 %all-gather.6.cloned.1.call-start = ((), (), s32[]{:S(2)}) async-start(), calls=%async_computation.1 | async-start | bytes 6963200 | tf_op jit(solution)/shard_map/all_gather | solution.py:36
  7.3 132.7 %all-gather.4.cloned.1.call-start = ((), (), s32[]{:S(2)}) async-start(), calls=%async_computation | async-start | bytes 6963200 | tf_op jit(solution)/shard_map/all_gather | solution.py:35
  8.0 196.2 %all-gather.8.cloned.1.call-start = ((), (), s32[]{:S(2)}) async-start(), calls=%async_computation.2 | async-start | bytes 6963200 | tf_op jit(solution)/shard_map/all_gather | solution.py:37
  12.2 127.8 %copy-start.4 = (f32[3200]{0:T(1024)S(1)}, f32[3200]{0:T(1024)}, u32[]{:S(2)}) copy-start(f32[3200]{0:T(1024)} %param.9) | copy-start | bytes 38404
  86.5 69.2 %copy-start.1 = (f32[1024]{0:T(1024)S(1)}, f32[1024]{0:T(1024)}, u32[]{:S(2)}) copy-start(f32[1024]{0:T(1024)} %param.14) | copy-start | bytes 12292
  157.9 68.0 %copy-start.3 = (s32[768]{0:T(1024)S(1)}, s32[768]{0:T(1024)}, u32[]{:S(2)}) copy-start(s32[768]{0:T(1024)} %param.15) | copy-start | bytes 9220
  157.9 275.1 %copy-start.2 = (f32[1024]{0:T(1024)S(1)}, f32[1024]{0:T(1024)}, u32[]{:S(2)}) copy-start(f32[1024]{0:T(1024)} %param.13) | copy-start | bytes 12292
  215.7 219.6 %collective-permute-start.4 = (bf16[768,2048]{1,0:T(8,128)(2,1)}, bf16[768,2048]{1,0:T(8,128)(2,1)}, u32[]{:S(2)}, u32[]{:S(2)}) collective-permute-start(bf16[768,2048]{1,0:T(8,128)(2,1)} %pad_maximum_fusion), channel_id=1, source_target_pairs={{0,2},{1,3},{2,4},{3,5},{4,6},{5,7},{6,8},{7,9},{8,10},{9,11},{10,... | collective-permute-start | bytes 9437192 | tf_op jit(solution)/shard_map/ppermute | solution.py:19
  219.8 217.7 %collective-permute-start.5 = (bf16[768,2048]{1,0:T(8,128)(2,1)}, bf16[768,2048]{1,0:T(8,128)(2,1)}, u32[]{:S(2)}, u32[]{:S(2)}) collective-permute-start(bf16[768,2048]{1,0:T(8,128)(2,1)} %pad_maximum_fusion), channel_id=1, source_target_pairs={{0,1},{1,2},{2,3},{3,4},{4,5},{5,6},{6,7},{7,8},{8,9},{9,10},{10,1... | collective-permute-start | bytes 9437192 | tf_op jit(solution)/shard_map/ppermute | solution.py:19
  223.3 216.8 %collective-permute-start.6 = (bf16[768,2048]{1,0:T(8,128)(2,1)}, bf16[768,2048]{1,0:T(8,128)(2,1)}, u32[]{:S(2)}, u32[]{:S(2)}) collective-permute-start(bf16[768,2048]{1,0:T(8,128)(2,1)} %pad_maximum_fusion), channel_id=1, source_target_pairs={{1,0},{2,1},{3,2},{4,3},{5,4},{6,5},{7,6},{8,7},{9,8},{10,9},{11,1... | collective-permute-start | bytes 9437192 | tf_op jit(solution)/shard_map/ppermute | solution.py:19
  224.6 217.8 %collective-permute-start.7 = (bf16[768,2048]{1,0:T(8,128)(2,1)}, bf16[768,2048]{1,0:T(8,128)(2,1)}, u32[]{:S(2)}, u32[]{:S(2)}) collective-permute-start(bf16[768,2048]{1,0:T(8,128)(2,1)} %pad_maximum_fusion), channel_id=1, source_target_pairs={{2,0},{3,1},{4,2},{5,3},{6,4},{7,5},{8,6},{9,7},{10,8},{11,9},{12,... | collective-permute-start | bytes 9437192 | tf_op jit(solution)/shard_map/ppermute | solution.py:19
  225.9 162.0 %collective-permute-start = (bf16[768]{0:T(1024)(128)(2,1)S(1)}, bf16[768]{0:T(1024)(128)(2,1)S(1)}, u32[]{:S(2)}, u32[]{:S(2)}) collective-permute-start(bf16[768]{0:T(1024)(128)(2,1)S(1)} %add_convert_fusion), channel_id=1, source_target_pairs={{0,2},{1,3},{2,4},{3,5},{4,6},{5,7},{6,8},{7,9},{8,10},{9,11},{10,... | collective-permute-start | bytes 4616 | tf_op jit(solution)/shard_map/ppermute | solution.py:19
  388.0 35.9 %collective-permute-start.1 = (bf16[768]{0:T(1024)(128)(2,1)S(1)}, bf16[768]{0:T(1024)(128)(2,1)S(1)}, u32[]{:S(2)}, u32[]{:S(2)}) collective-permute-start(bf16[768]{0:T(1024)(128)(2,1)S(1)} %add_convert_fusion), channel_id=1, source_target_pairs={{0,1},{1,2},{2,3},{3,4},{4,5},{5,6},{6,7},{7,8},{8,9},{9,10},{10,1... | collective-permute-start | bytes 4616 | tf_op jit(solution)/shard_map/ppermute | solution.py:19
  423.9 3.0 collective-permute-start.2
  426.9 6.1 %collective-permute-start.3 = (bf16[768]{0:T(1024)(128)(2,1)S(1)}, bf16[768]{0:T(1024)(128)(2,1)S(1)}, u32[]{:S(2)}, u32[]{:S(2)}) collective-permute-start(bf16[768]{0:T(1024)(128)(2,1)S(1)} %add_convert_fusion), channel_id=1, source_target_pairs={{2,0},{3,1},{4,2},{5,3},{6,4},{7,5},{8,6},{9,7},{10,8},{11,9},{12,... | collective-permute-start | bytes 4616 | tf_op jit(solution)/shard_map/ppermute | solution.py:19
  444.6 34.8 %copy-start = (bf16[3840,2048]{1,0:T(8,128)(2,1)}, bf16[3840,2048]{1,0:T(8,128)(2,1)S(1)}, u32[]{:S(2)}) copy-start(bf16[3840,2048]{1,0:T(8,128)(2,1)S(1)} %constant_dynamic-update-slice_fusion) | copy-start | bytes 47185924
Sparse Core Ops, SparseCore 0:
  9.6 66.0 all-gather.5
  78.0 61.8 all-gather.3
  142.2 61.9 all-gather.7
where the time goes:
time: 605 us; the launch traced here: 596 us
  waiting for transfers between devices  329 us (54%)
  matrix products  129 us (21%)
  other arithmetic  54.2 us (9%)
  starting transfers between devices  53 us (9%)
  between operations  13.8 us (2%)
  local copies, waits for them, and re-layouts  11.5 us (2%)
    ppermute x8, waiting for transfers between devices, from_behind(): return lax.ppermute(shard, axis, pairs)  164 us
    all_gather x1, waiting for transfers between devices, on_device(): key_part = add_rows(lax.all_gather(w_key, 'seq', axis=0, tiled=True))  63.6 us
    dot_general x8, matrix products, on_device(): jnp.dot(weights, v_head, preferred_element_type=jnp.float32)  54.4 us
    all_gather x1, waiting for transfers between devices, on_device(): queries = add_rows(lax.all_gather(w_query, 'seq', axis=0, tiled=True))  53.4 us
    ppermute x8, starting transfers between devices, from_behind(): return lax.ppermute(shard, axis, pairs)  52.9 us
    all_gather x1, waiting for transfers between devices, on_device(): value_part = add_rows(lax.all_gather(w_value, 'seq', axis=0, tiled=True))  46.3 us
    reduce_sum x8, other arithmetic, on_device(): weights = (expo / jnp.sum(expo, axis=1, keepdims=True)).astype(jnp.bfloat16)  44 us
    dot_general x8, matrix products, on_device(): jnp.einsum('qd,kd->qk', q_head, k_head, preferred_element_type=jnp.float32)  43.9 us
  transfers between devices with their start and end apart: 11, of which 7 were waited for; matrix products, arithmetic and copies ran while one was open for 6% of the time, Pallas kernels for 0%

commit v1 on v0

v1 whole, which is shorter than its diff:
```python
import functools
import math

import jax
import jax.numpy as jnp
from jax import lax
from jax.experimental import pallas as pl
from jax.experimental.pallas import tpu as pltpu
from jax.sharding import PartitionSpec as P

HEADS = 16
HEAD_DIM = 128
MOST = 1025
EPS = 1e-06
GROUP = 4
CHUNKS = 4
BLOCK = 256
MESH = pl.DeviceIdType.MESH
ANY = pl.BlockSpec(memory_space=pl.ANY)


def greet(partners):
    barrier = pltpu.get_barrier_semaphore()
    count = 0
    for device, there in partners:
        if there is None:
            pl.semaphore_signal(barrier, inc=1, device_id=device, device_id_type=MESH)
            count = count + 1
        else:

            @pl.when(there)
            def _(device=device):
                pl.semaphore_signal(barrier, inc=1, device_id=device, device_id_type=MESH)

            count = count + there.astype(jnp.int32)
    pl.semaphore_wait(barrier, count)


def remote(src, dst, send, recv, device):
    return pltpu.make_async_remote_copy(
        src_ref=src, dst_ref=dst, send_sem=send, recv_sem=recv,
        device_id=device, device_id_type=MESH,
    )


def gather_kernel(planes, n_ref, w_ref, x_out, w_out, own_sem, core_s, core_r, y_s, y_r, x_s, x_r,
                  cf_s, cf_r, a_s, a_r, up_s, up_r, down_s, down_r):
    h = lax.axis_index("head")
    s = lax.axis_index("seq")
    z, g = s // GROUP, s % GROUP
    y, c = g // 2, g % 2
    base = z * GROUP
    core_g = y * 2 + (1 - c)
    far_g = (1 - y) * 2 + c
    core_dev, y_dev, x_dev = (h, base + core_g), (h, base + far_g), (1 - h, s)
    up_dev = (h, jnp.minimum(s + GROUP, planes * GROUP - 1))
    down_dev = (h, jnp.maximum(s - GROUP, 0))
    has_up, has_down = z < planes - 1, z > 0
    group_dev = [(h, base + (g + d) % GROUP) for d in range(GROUP)]
    greet([(x_dev, None)] + [(group_dev[d], None) for d in range(1, GROUP)]
          + [(up_dev, has_up), (down_dev, has_down)])

    rows = n_ref.shape[0]
    half = rows // 2
    piece = half // CHUNKS

    def spread(d):
        return remote(w_ref.at[(g + d) % GROUP], w_out.at[s], a_s.at[d], a_r.at[d], group_dev[d])

    def climb(t, j):
        slot = (z - t) * GROUP + (g + GROUP - j) % GROUP
        src = w_ref.at[g] if (t, j) == (0, 0) else w_out.at[slot]
        return remote(src, w_out.at[slot], up_s.at[t * GROUP + j], up_r.at[t * GROUP + j], up_dev)

    def sink(t, j):
        slot = (z + t) * GROUP + (g + GROUP - j) % GROUP
        src = w_ref.at[g] if (t, j) == (0, 0) else w_out.at[slot]
        return remote(src, w_out.at[slot], down_s.at[t * GROUP + j], down_r.at[t * GROUP + j], down_dev)

    def any_slot(sem_s, sem_r, device):
        return remote(w_out.at[0], w_out.at[0], sem_s, sem_r, device)

    def token_rows(block, which, k):
        return x_out.at[block, pl.ds(pl.multiple_of(which * half + k * piece, 16), piece)]

    def over_y(k):
        first = pl.multiple_of(h * half + k * piece, 16)
        return remote(n_ref.at[pl.ds(first, piece)], token_rows(g, h, k), y_s.at[k], y_r.at[k], y_dev)

    def over_x(k):
        part = token_rows(far_g, h, k)
        return remote(part, part, x_s.at[k], x_r.at[k], x_dev)

    def over_core(k, from_x):
        part = token_rows(far_g, 1 - h if from_x else h, k)
        i = CHUNKS + k if from_x else k
        return remote(part, part, cf_s.at[i], cf_r.at[i], core_dev)

    own_w = pltpu.make_async_copy(w_ref.at[g], w_out.at[s], own_sem.at[0])
    own_x = pltpu.make_async_copy(n_ref, x_out.at[g], own_sem.at[1])
    block_core = remote(n_ref, x_out.at[g], core_s, core_r, core_dev)

    def send_z(t, j):
        @pl.when(jnp.logical_and(has_up, z - t >= 0))
        def _():
            climb(t, j).start()

        @pl.when(jnp.logical_and(has_down, z + t <= planes - 1))
        def _():
            sink(t, j).start()

    def take_z(t, j):
        i = t * GROUP + j

        @pl.when(z - 1 - t >= 0)
        def _():
            any_slot(up_s.at[i], up_r.at[i], down_dev).wait_recv()

        @pl.when(z + 1 + t <= planes - 1)
        def _():
            any_slot(down_s.at[i], down_r.at[i], up_dev).wait_recv()

        if t + 1 <= planes - 2:
            send_z(t + 1, j)

    send_z(0, 0)
    for d in (2, 1, 3):
        spread(d).start()
    for k in range(CHUNKS):
        over_y(k).start()
    block_core.start()
    own_w.start()
    own_x.start()
    for d in range(1, GROUP):
        spread(d).wait_recv()
        send_z(0, d)

    def take_y(k):
        over_y(k).wait_recv()
        over_x(k).start()
        over_core(k, False).start()

    def take_x(k):
        over_x(k).wait_recv()
        over_core(k, True).start()

    for k in range(CHUNKS):
        for j in range(k * GROUP // CHUNKS, (k + 1) * GROUP // CHUNKS):
            take_z(0, j)
        take_y(k)
        if k >= 1:
            take_x(k - 1)
        if k >= 2:
            take_z(1, k - 2)
    for j in range(CHUNKS - 2, GROUP):
        take_z(1, j)
    take_x(CHUNKS - 1)
    for t in range(2, planes - 1):
        for j in range(GROUP):
            take_z(t, j)

    own_w.wait()
    own_x.wait()
    block_core.wait()
    for k in range(CHUNKS):
        over_y(k).wait_send()
        over_x(k).wait_send()
        over_core(k, False).wait()
        over_core(k, True).wait()
    for d in range(1, GROUP):
        spread(d).wait_send()
    for t in range(planes - 1):
        for j in range(GROUP):

            @pl.when(jnp.logical_and(has_up, z - t >= 0))
            def _():
                climb(t, j).wait_send()

            @pl.when(jnp.logical_and(has_down, z + t <= planes - 1))
            def _():
                sink(t, j).wait_send()


def gather_plane(planes, normed, wcat):
    rows, width = normed.shape
    _, w_rows, w_cols = wcat.shape
    dma = pltpu.SemaphoreType.DMA
    hops = (planes - 1) * GROUP
    return pl.pallas_call(
        functools.partial(gather_kernel, planes),
        out_shape=(
            jax.ShapeDtypeStruct((GROUP, rows, width), normed.dtype),
            jax.ShapeDtypeStruct((planes * GROUP, w_rows, w_cols), wcat.dtype),
        ),
        in_specs=[ANY, ANY],
        out_specs=(ANY, ANY),
        scratch_shapes=[
            dma((2,)), dma, dma, dma((CHUNKS,)), dma((CHUNKS,)), dma((CHUNKS,)), dma((CHUNKS,)),
            dma((2 * CHUNKS,)), dma((2 * CHUNKS,)), dma((GROUP,)), dma((GROUP,)),
            dma((hops,)), dma((hops,)), dma((hops,)), dma((hops,)),
        ],
        compiler_params=pltpu.CompilerParams(collective_id=0, has_side_effects=True),
        name="gather_plane",
    )(normed, wcat)


def sums_kernel(part_ref, out_ref, slots, send, recv):
    h = lax.axis_index("head")
    s = lax.axis_index("seq")
    g = s % GROUP
    base = s - g
    others = []
    for dh in range(2):
        for d in range(GROUP):
            if (dh, d) != (0, 0):
                others.append((((h + dh) % 2, base + (g + d) % GROUP), dh * GROUP + d))
    greet([(device, None) for device, _ in others])
    mine = h * GROUP + g
    copies = []
    for device, i in others:
        copy = remote(part_ref, slots.at[mine], send.at[i], recv.at[i], device)
        copy.start()
        copies.append(copy)
    slots[mine] = part_ref[...]
    for copy in copies:
        copy.wait()
    total = slots[0]
    for i in range(1, 2 * GROUP):
        total = total + slots[i]
    out_ref[...] = total


def plane_sums(part):
    count = 2 * GROUP
    return pl.pallas_call(
        sums_kernel,
        out_shape=jax.ShapeDtypeStruct(part.shape, part.dtype),
        in_specs=[pl.BlockSpec(memory_space=pltpu.VMEM)],
        out_specs=pl.BlockSpec(memory_space=pltpu.VMEM),
        scratch_shapes=[
            pltpu.VMEM((count,) + part.shape, part.dtype),
            pltpu.SemaphoreType.DMA((count,)),
            pltpu.SemaphoreType.DMA((count,)),
        ],
        compiler_params=pltpu.CompilerParams(collective_id=1, has_side_effects=True),
        name="plane_sums",
    )(part)


def return_kernel(a_ref, o_ref, own, send, recv):
    h = lax.axis_index("head")
    s = lax.axis_index("seq")
    g = s % GROUP
    base = s - g
    width = a_ref.shape[2]
    greet([((h, base + (g + d) % GROUP), None) for d in range(1, GROUP)])
    columns = o_ref.at[:, pl.ds(pl.multiple_of(g * width, 128), width)]
    copies = []
    for d in (2, 3, 1):
        to = (g + d) % GROUP
        copy = remote(a_ref.at[to], columns, send.at[d], recv.at[d], (h, base + to))
        copy.start()
        copies.append(copy)
    here = pltpu.make_async_copy(a_ref.at[g], columns, own)
    here.start()
    here.wait()
    for copy in copies:
        copy.wait()


def return_tokens(attended):
    group, rows, width = attended.shape
    dma = pltpu.SemaphoreType.DMA
    return pl.pallas_call(
        return_kernel,
        out_shape=jax.ShapeDtypeStruct((rows, group * width), attended.dtype),
        in_specs=[ANY],
        out_specs=ANY,
        scratch_shapes=[dma, dma((GROUP,)), dma((GROUP,))],
        compiler_params=pltpu.CompilerParams(collective_id=2, has_side_effects=True),
        name="return_tokens",
    )(attended)


def attention_kernel(span_ref, q_ref, k_ref, v_ref, qm_ref, km_ref, o_ref, s_buf, m_buf, l_buf):
    block = pl.program_id(0)
    first, last = span_ref[0, block], span_ref[1, block]
    heads = q_ref.shape[1] // HEAD_DIM
    rate = math.log2(math.e) / math.sqrt(HEAD_DIM)
    own = jnp.broadcast_to(qm_ref[...], (BLOCK, BLOCK))
    for head in range(heads):
        cols = slice(head * HEAD_DIM, (head + 1) * HEAD_DIM)
        q = q_ref[:, cols]

        def lanes(x, op):
            out = x[:, :128]
            for i in range(1, BLOCK // 128):
                out = op(out, x[:, i * 128 : (i + 1) * 128])
            return out

        def score(b, highest):
            keys = k_ref[pl.ds(pl.multiple_of(b * BLOCK, BLOCK), BLOCK), cols]
            s = lax.dot_general(q, keys, (((1,), (1,)), ((), ())), preferred_element_type=jnp.float32)
            s = jnp.where(own == km_ref[b], s, -1e30)
            s_buf[b - first] = s
            return jnp.maximum(highest, lanes(s, jnp.maximum))

        highest = lax.fori_loop(first, last, score, jnp.full((BLOCK, 128), -1e30, jnp.float32))
        m = jnp.max(highest, axis=1, keepdims=True)

        def expo(b, total):
            e = jnp.exp2((s_buf[b - first] - m) * rate)
            s_buf[b - first] = e
            return total + lanes(e, jnp.add)

        total = lax.fori_loop(first, last, expo, jnp.zeros((BLOCK, 128), jnp.float32))
        share = 1.0 / jnp.sum(total, axis=1, keepdims=True)

        def mix(b, acc):
            w = (s_buf[b - first] * share).astype(jnp.bfloat16)
            values = v_ref[pl.ds(pl.multiple_of(b * BLOCK, BLOCK), BLOCK), cols]
            return acc + jnp.dot(w, values, preferred_element_type=jnp.float32)

        acc = lax.fori_loop(first, last, mix, jnp.zeros((BLOCK, HEAD_DIM), jnp.float32))
        o_ref[:, cols] = acc.astype(o_ref.dtype)


def attention(q_hat, near_k, near_v, own_marks, near_marks):
    rows, width = q_hat.shape
    near = near_k.shape[0]
    blocks, key_blocks = rows // BLOCK, near // BLOCK
    first_mark = own_marks[::BLOCK]
    last_mark = own_marks[BLOCK - 1 :: BLOCK]
    lowest = jnp.sum((near_marks[None, :] < first_mark[:, None]).astype(jnp.int32), axis=1)
    highest = jnp.sum((near_marks[None, :] <= last_mark[:, None]).astype(jnp.int32), axis=1)
    span = jnp.stack([lowest // BLOCK, (highest + BLOCK - 1) // BLOCK])
    most = min(key_blocks, (BLOCK + 2 * (MOST - 1)) // BLOCK + 1)
    pairs = rows * (BLOCK * 4) * (width // HEAD_DIM)
    return pl.pallas_call(
        attention_kernel,
        grid_spec=pltpu.PrefetchScalarGridSpec(
            num_scalar_prefetch=1,
            grid=(blocks,),
            in_specs=[
                pl.BlockSpec((BLOCK, width), lambda i, span: (i, 0)),
                pl.BlockSpec(memory_space=pltpu.VMEM),
                pl.BlockSpec(memory_space=pltpu.VMEM),
                pl.BlockSpec((BLOCK, 1), lambda i, span: (i, 0)),
                pl.BlockSpec(memory_space=pltpu.VMEM),
            ],
            out_specs=pl.BlockSpec((BLOCK, width), lambda i, span: (i, 0)),
            scratch_shapes=[
                pltpu.VMEM((most, BLOCK, BLOCK), jnp.float32),
                pltpu.VMEM((BLOCK, 128), jnp.float32),
                pltpu.VMEM((BLOCK, 128), jnp.float32),
            ],
        ),
        out_shape=jax.ShapeDtypeStruct((rows, width), jnp.bfloat16),
        compiler_params=pltpu.CompilerParams(vmem_limit_bytes=40 * 1024 * 1024),
        cost_estimate=pl.CostEstimate(
            flops=pairs * HEAD_DIM * 4, bytes_accessed=near * width * 4 + rows * width * 4,
            transcendentals=pairs),
        name="tile_attention",
    )(span, q_hat, near_k, near_v, own_marks[:, None], near_marks.reshape(key_blocks, 1, BLOCK))


def from_behind(shard, by):
    size = lax.axis_size("seq")
    pairs = [(i, i + by) for i in range(size) if 0 <= i + by < size]
    return lax.ppermute(shard, "seq", pairs)


def with_halo(shard, step):
    rows_here = shard.shape[0]
    left, right, need, distance = [], [], MOST - 1, 1
    while need > 0:
        take = min(need, rows_here)
        left.insert(0, from_behind(shard[rows_here - take :], distance * step))
        right.append(from_behind(shard[:take], -distance * step))
        need, distance = need - take, distance + 1
    return jnp.concatenate(left + [shard] + right, axis=0)


def on_device(grouped, tokens, ln_gain, w_query, w_key, w_value, q_gain, k_gain, seg_ids):
    heads_here = w_query.shape[1] // HEAD_DIM
    total_channels = HEADS * HEAD_DIM
    place = lax.axis_index("seq")
    seq = lax.axis_size("seq")
    margin = MOST - 1
    all_marks = lax.all_gather(seg_ids, "seq", axis=0, tiled=True)
    floats = tokens.astype(jnp.float32)
    normed = (
        floats * lax.rsqrt(jnp.mean(floats * floats, axis=1, keepdims=True) + EPS) * ln_gain
    ).astype(jnp.bfloat16)
    if grouped:
        share = w_query.shape[1] // GROUP
        step = GROUP
        member = place % GROUP
        wcat = jnp.concatenate(
            [w.reshape(w.shape[0], GROUP, share) for w in (w_key, w_value, w_query)], axis=2
        ).transpose(1, 0, 2)
        near_tokens, weights = gather_plane(seq // GROUP, normed, wcat)
        rows = GROUP * tokens.shape[0]
        near_tokens = near_tokens.reshape(rows, tokens.shape[1])
        weights = weights.reshape(tokens.shape[1], 3 * share)
        w_k, w_v, w_q = (weights[:, i * share : (i + 1) * share] for i in range(3))
        q_gain = lax.dynamic_slice_in_dim(q_gain, member * share, share)
        k_gain = lax.dynamic_slice_in_dim(k_gain, member * share, share)
    else:
        step = 1
        rows = tokens.shape[0]
        near_tokens = normed
        w_k, w_v, w_q = (
            lax.all_gather(w, "seq", axis=0, tiled=True) for w in (w_key, w_value, w_query)
        )

    def project(w):
        return jnp.dot(near_tokens, w, preferred_element_type=jnp.float32)

    def norm(part, gain):
        square = jnp.sum(part * part, axis=1)
        if grouped:
            square = plane_sums(square.reshape(rows // 128, 128)).reshape(rows)
        else:
            square = lax.psum(square, "head")
        return (part * lax.rsqrt(square[:, None] / total_channels + EPS) * gain).astype(jnp.bfloat16)

    near_v = with_halo(project(w_v).astype(jnp.bfloat16), step)
    near_k = with_halo(norm(project(w_k), k_gain), step)
    q_hat = norm(project(w_q), q_gain)

    low = jnp.full((margin,), -1, jnp.int32)
    high = jnp.full((margin,), jnp.iinfo(jnp.int32).max, jnp.int32)
    padded = jnp.concatenate([low, all_marks, high])
    first = place // step * rows
    near_marks = lax.dynamic_slice_in_dim(padded, first, rows + 2 * margin)
    own_marks = lax.slice_in_dim(near_marks, margin, margin + rows)
    attended = attention(q_hat, near_k, near_v, own_marks, near_marks)
    if grouped:
        attended = return_tokens(attended.reshape(GROUP, tokens.shape[0], attended.shape[1]))
    return attended


def solution(mesh):
    seq, heads = mesh.shape["seq"], mesh.shape["head"]
    grouped = heads == 2 and seq % GROUP == 0 and HEADS // heads % GROUP == 0
    return jax.shard_map(
        functools.partial(on_device, grouped),
        mesh=mesh,
        in_specs=(
            P("seq", None),
            P(),
            P("seq", "head"),
            P("seq", "head"),
            P("seq", "head"),
            P("head"),
            P("head"),
            P("seq"),
        ),
        out_specs=P("seq", "head"),
        check_vma=False,
    )
```

time: 605 us -> 362 us (0.60)
  waiting for transfers between devices: 329 us -> 0.01 us
  Pallas kernels: 0 us -> 252 us
  matrix products: 129 us -> 33.5 us
  starting transfers between devices: 53 us -> 13.3 us
  other arithmetic: 54.2 us -> 20.4 us
  blocking collectives: 4.97 us -> 25.6 us
  between operations: 13.8 us -> 0.26 us
    pallas_call x0 -> x5, Pallas kernels: none -> 252 us  [the longest x1 163 us: gather_plane(): pl.pallas_call(functools.partial(gather_kernel, planes), out_shape=(jax.S...]
    ppermute x8 -> x4, waiting for transfers between devices: 164 us -> 0.01 us  [from_behind(): return lax.ppermute(shard, 'seq', pairs)]
    all_gather x3 -> x0, waiting for transfers between devices: 163 us -> none  [the longest x1 63.6 us: on_device(): key_part = add_rows(lax.all_gather(w_key, 'seq', axis=0, tiled=True))]
    dot_general x19 -> x3, matrix products: 129 us -> 33.5 us  [project(): return jnp.dot(near_tokens, w, preferred_element_type=jnp.float32)]
    reduce_sum x8 -> x1, other arithmetic: 44 us -> 0.27 us  [attention(): jnp.sum((near_marks[None, :] < first_mark[:, None]).astype(jnp.int32), ax...]
    ppermute x8 -> x4, starting transfers between devices: 52.9 us -> 13.3 us  [from_behind(): return lax.ppermute(shard, 'seq', pairs)]
    all_gather x0 -> x1, blocking collectives: none -> 25.6 us  [on_device(): all_marks = lax.all_gather(seg_ids, 'seq', axis=0, tiled=True)]
    convert_element_type x3, other arithmetic: 4.46 us -> 11.2 us  [the longest x1 6.47 us: on_device(): normed = (floats * lax.rsqrt(jnp.mean(floats * floats, axis=1, keepdims=T...]
  transfers between devices with their start and end apart: 11 -> 4, of which waited for: 7 -> 0; matrix products, arithmetic and copies ran while one was open for 6% -> 9% of each run, Pallas kernels for 0% -> 2%
where the time goes in v1:
time: 362 us; the launch traced here: 358 us
  Pallas kernels  252 us (70%)
  matrix products  33.5 us (9%)
  blocking collectives  25.6 us (7%)
  other arithmetic  20.4 us (6%)
  starting transfers between devices  13.3 us (4%)
  local copies, waits for them, and re-layouts  13.1 us (4%)
    pallas_call x1, Pallas kernels, gather_plane(): pl.pallas_call(functools.partial(gather_kernel, planes), out_shape=(jax.S...  163 us
    pallas_call x1, Pallas kernels, attention(): pl.pallas_call(attention_kernel, grid_spec=pltpu.PrefetchScalarGridSpec(n...  55.8 us
    dot_general x3, matrix products, project(): return jnp.dot(near_tokens, w, preferred_element_type=jnp.float32)  33.5 us
    all_gather x1, blocking collectives, on_device(): all_marks = lax.all_gather(seg_ids, 'seq', axis=0, tiled=True)  25.6 us
    pallas_call x1, Pallas kernels, return_tokens(): pl.pallas_call(return_kernel, out_shape=jax.ShapeDtypeStruct((rows, group...  19.8 us
    ppermute x4, starting transfers between devices, from_behind(): return lax.ppermute(shard, 'seq', pairs)  13.3 us
    pallas_call x2, Pallas kernels, plane_sums(): pl.pallas_call(sums_kernel, out_shape=jax.ShapeDtypeStruct(part.shape, pa...  12.7 us
  transfers between devices with their start and end apart: 4, of which 0 were waited for; matrix products, arithmetic and copies ran while one was open for 9% of the time, Pallas kernels for 2%

profile of v1, /device:TPU:0, one launch (start us, length us, event | category | flops | bytes accessed | tf_op | source)
XLA Modules:
  0.0 357.7 jit_solution(8134415104218387925)
XLA Ops:
  0.0 3.5 fusion
  3.6 6.5 %fusion.2.n_ref = bf16[768,3200]{1,0:T(8,128)(2,1)} fusion(bf16[768,3200]{1,0:T(8,128)(2,1)} %param.8, f32[3200]{0:T(1024)S(1)} %copy-done.6, f32[768]{0:T(1024)S(1)} %add_rsqrt_fusion), kind=kLoop, calls=%fused_computation.4 | loop fusion | flops 9830400 | bytes 9846272 | tf_op jit(solution)/shard_map/convert_element_type | solution.py:394
  10.1 1.1 maximum_bitcast_fusion.w_ref
  11.2 163.2 %gather_plane.1 = (bf16[4,768,3200]{2,1,0:T(8,128)(2,1)}, bf16[16,200,768]{2,1,0:T(8,128)(2,1)}) custom-call(bf16[768,3200]{1,0:T(8,128)(2,1)} %fusion.2.n_ref, bf16[4,200,768]{2,1,0:T(8,128)(2,1)} %maximum_bitcast_fusion.w_ref), custom_call_target="tpu_custom_call" | custom-call | tf_op jit(solution)/shard_map/gather_plane/pallas_call | solution.py:189
  174.4 11.8 %multiply_reduce_fusion = (f32[3072]{0:T(1024)}, f32[3072,256]{1,0:T(8,128)}) fusion(bf16[3072,3200]{1,0:T(8,128)(2,1)} %bitcast.53, bf16[3200,768]{1,0:T(8,128)(2,1)} %bitcast.56), kind=kOutput, calls=%fused_computation.7 | convolution fusion | flops 5034734592 | bytes 24457216 | tf_op jit(solution)/shard_map/dot_general | solution.py:418
  186.2 6.4 %plane_sums.3 = f32[24,128]{1,0:T(8,128)} custom-call(f32[24,128]{1,0:T(8,128)} %bitcast.52), custom_call_target="tpu_custom_call" | custom-call | tf_op jit(solution)/shard_map/plane_sums/pallas_call | solution.py:235
  192.7 0.7 rsqrt_bitcast_fusion
  193.4 0.8 dynamic_slice.11
  194.1 2.4 multiply_convert_fusion
  196.5 1.1 fusion.11
  197.6 1.3 collective-permute-start.1
  198.9 5.4 %collective-permute-start = (bf16[1024,256]{1,0:T(8,128)(2,1)}, bf16[1024,256]{1,0:T(8,128)(2,1)}, u32[]{:S(2)}, u32[]{:S(2)}) collective-permute-start(bf16[1024,256]{1,0:T(8,128)(2,1)} %get-tuple-element.13), channel_id=1, source_target_pairs={{0,4},{1,5},{2,6},{3,7},{4,8},{5,9},{6,10},{7,11},{8,12},{9,13},{1... | collective-permute-start | bytes 1572872 | tf_op jit(solution)/shard_map/ppermute | solution.py:370
  204.3 9.9 %convolution_convert_fusion = bf16[3072,256]{1,0:T(8,128)(2,1)S(1)} fusion(bf16[3072,3200]{1,0:T(8,128)(2,1)} %bitcast.54, bf16[3200,768]{1,0:T(8,128)(2,1)} %bitcast.57), kind=kOutput, calls=%fused_computation.5 | convolution fusion | flops 5033951232 | bytes 22872064 | tf_op jit(solution)/shard_map/dot_general | solution.py:418
  214.2 1.1 copy-done.1
  215.3 1.1 fusion.10
  216.4 1.3 collective-permute-start.3
  217.7 5.4 %collective-permute-start.2 = (bf16[1024,256]{1,0:T(8,128)(2,1)}, bf16[1024,256]{1,0:T(8,128)(2,1)}, u32[]{:S(2)}, u32[]{:S(2)}) collective-permute-start(bf16[1024,256]{1,0:T(8,128)(2,1)} %get-tuple-element.11), channel_id=1, source_target_pairs={{0,4},{1,5},{2,6},{3,7},{4,8},{5,9},{6,10},{7,11},{8,12},{9,13},{1... | collective-permute-start | bytes 1572872 | tf_op jit(solution)/shard_map/ppermute | solution.py:370
  223.1 25.6 %all-gather = s32[16,1,768]{2,1,0:T(1,128)S(1)} all-gather(s32[1,1,768]{2,1,0:T(1,128)S(1)} %reshape.185), channel_id=1, replica_groups=mesh['head'=2,'seq'=16] {'seq'}, dimensions={0}, use_global_device_ids=true | all-gather | bytes 52224 | tf_op jit(solution)/shard_map/all_gather | solution.py:390
  248.9 11.7 %multiply_reduce_fusion.1 = (f32[3072]{0:T(1024)}, f32[3072,256]{0,1:T(8,128)}) fusion(bf16[3072,3200]{1,0:T(8,128)(2,1)} %bitcast.55, bf16[3200,768]{1,0:T(8,128)(2,1)} %bitcast.58), kind=kOutput, calls=%fused_computation.9 | convolution fusion | flops 5034734592 | bytes 24457216 | tf_op jit(solution)/shard_map/dot_general | solution.py:418
  260.6 3.5 copy.23
  264.2 0.8 dynamic_slice.10
  264.9 6.3 %plane_sums.2 = f32[24,128]{1,0:T(8,128)} custom-call(f32[24,128]{1,0:T(8,128)} %bitcast.51), custom_call_target="tpu_custom_call" | custom-call | tf_op jit(solution)/shard_map/plane_sums/pallas_call | solution.py:235
  271.3 0.7 rsqrt_bitcast_fusion.1
  272.0 0.5 copy.24.qm_ref
  272.5 0.3 convert_reduce_fusion.1
  272.8 2.4 multiply_convert_fusion.1.q_ref
  275.2 1.5 pad_maximum_fusion.k_ref
  276.9 1.4 pad_maximum_fusion.1.v_ref
  278.3 55.8 %tile_attention.1 = bf16[3072,256]{1,0:T(8,128)(2,1)S(1)} custom-call(s32[2,12]{1,0:T(2,128)S(1)} %pad_add_fusion.span_ref, bf16[3072,256]{1,0:T(8,128)(2,1)S(1)} %multiply_convert_fusion.1.q_ref, bf16[5120,256]{1,0:T(8,128)(2,1)S(1)} %pad_maximum_fusion.k_ref, bf16[5120,256]{1,0:T(8,128)(2,1)S(1)} %pad_maximum_fusion.1.v_ref, s32[3072,1]{1,0:T(8,128)S(1)} %copy.24.qm_ref, ...), custom_call_target="tpu_custom_call" | custom-call | flops 3221225472 | bytes 8388608 | tf_op jit(solution)/shard_map/tile_attention/pallas_call | solution.py:339
  334.1 1.1 copy-done
  335.3 19.8 %return_tokens.1 = bf16[768,1024]{1,0:T(8,128)(2,1)} custom-call(bf16[4,768,256]{2,1,0:T(8,128)(2,1)} %bitcast.43), custom_call_target="tpu_custom_call" | custom-call | tf_op jit(solution)/shard_map/return_tokens/pallas_call | solution.py:274
  355.1 2.7 copy.33
  (30 shorter events, 0.6 us)
Async XLA Ops:
  0.0 3.5 copy-start.3
  0.0 3.5 copy-start.6
  3.6 6.5 %copy-start.4 = (bf16[200,1024]{1,0:T(8,128)(2,1)S(1)}, bf16[200,1024]{1,0:T(8,128)(2,1)}, u32[]{:S(2)}) copy-start(bf16[200,1024]{1,0:T(8,128)(2,1)} %param.10) | copy-start | bytes 1228804
  3.6 6.5 %copy-start.5 = (bf16[200,1024]{1,0:T(8,128)(2,1)S(1)}, bf16[200,1024]{1,0:T(8,128)(2,1)}, u32[]{:S(2)}) copy-start(bf16[200,1024]{1,0:T(8,128)(2,1)} %param.12) | copy-start | bytes 1228804
  197.6 77.6 %collective-permute-start.1 = (bf16[1024,256]{1,0:T(8,128)(2,1)}, bf16[1024,256]{1,0:T(8,128)(2,1)}, u32[]{:S(2)}, u32[]{:S(2)}) collective-permute-start(bf16[1024,256]{1,0:T(8,128)(2,1)} %get-tuple-element.14), channel_id=1, source_target_pairs={{4,0},{5,1},{6,2},{7,3},{8,4},{9,5},{10,6},{11,7},{12,8},{13,9},{1... | collective-permute-start | bytes 1572872 | tf_op jit(solution)/shard_map/ppermute | solution.py:370
  198.8 24.2 %copy-start.7 = (s32[768]{0:T(1024)S(1)}, s32[768]{0:T(1024)}, u32[]{:S(2)}) copy-start(s32[768]{0:T(1024)} %param.15) | copy-start | bytes 9220
  198.9 76.4 %collective-permute-start = (bf16[1024,256]{1,0:T(8,128)(2,1)}, bf16[1024,256]{1,0:T(8,128)(2,1)}, u32[]{:S(2)}, u32[]{:S(2)}) collective-permute-start(bf16[1024,256]{1,0:T(8,128)(2,1)} %get-tuple-element.13), channel_id=1, source_target_pairs={{0,4},{1,5},{2,6},{3,7},{4,8},{5,9},{6,10},{7,11},{8,12},{9,13},{1... | collective-permute-start | bytes 1572872 | tf_op jit(solution)/shard_map/ppermute | solution.py:370
  214.2 1.1 copy-start.1
  216.4 60.3 %collective-permute-start.3 = (bf16[1024,256]{1,0:T(8,128)(2,1)}, bf16[1024,256]{1,0:T(8,128)(2,1)}, u32[]{:S(2)}, u32[]{:S(2)}) collective-permute-start(bf16[1024,256]{1,0:T(8,128)(2,1)} %get-tuple-element.12), channel_id=1, source_target_pairs={{4,0},{5,1},{6,2},{7,3},{8,4},{9,5},{10,6},{11,7},{12,8},{13,9},{1... | collective-permute-start | bytes 1572872 | tf_op jit(solution)/shard_map/ppermute | solution.py:370
  217.7 59.0 %collective-permute-start.2 = (bf16[1024,256]{1,0:T(8,128)(2,1)}, bf16[1024,256]{1,0:T(8,128)(2,1)}, u32[]{:S(2)}, u32[]{:S(2)}) collective-permute-start(bf16[1024,256]{1,0:T(8,128)(2,1)} %get-tuple-element.11), channel_id=1, source_target_pairs={{0,4},{1,5},{2,6},{3,7},{4,8},{5,9},{6,10},{7,11},{8,12},{9,13},{1... | collective-permute-start | bytes 1572872 | tf_op jit(solution)/shard_map/ppermute | solution.py:370
  275.2 1.7 copy-start.2
  334.1 1.1 copy-start

commit v2 on v1

--- a/solution.py
+++ b/solution.py
@@ -43,8 +43,8 @@
     )
 
 
-def gather_kernel(planes, n_ref, w_ref, x_out, w_out, own_sem, core_s, core_r, y_s, y_r, x_s, x_r,
-                  cf_s, cf_r, a_s, a_r, up_s, up_r, down_s, down_r):
+def gather_kernel(planes, n_ref, w_ref, m_ref, x_out, w_out, m_out, own_sem, core_s, core_r, y_s, y_r, x_s, x_r,
+                  cf_s, cf_r, a_s, a_r, up_s, up_r, down_s, down_r, mark_s, mark_r):
     h = lax.axis_index("head")
     s = lax.axis_index("seq")
     z, g = s // GROUP, s % GROUP
@@ -56,7 +56,8 @@
     up_dev = (h, jnp.minimum(s + GROUP, planes * GROUP - 1))
     down_dev = (h, jnp.maximum(s - GROUP, 0))
     has_up, has_down = z < planes - 1, z > 0
-    group_dev = [(h, base + (g + d) % GROUP) for d in range(GROUP)]
+    member = [(y + d // 2) % 2 * 2 + (c + d % 2) % 2 for d in range(GROUP)]
+    group_dev = [(h, base + m) for m in member]
     greet([(x_dev, None)] + [(group_dev[d], None) for d in range(1, GROUP)]
           + [(up_dev, has_up), (down_dev, has_down)])
 
@@ -65,15 +66,15 @@
     piece = half // CHUNKS
 
     def spread(d):
-        return remote(w_ref.at[(g + d) % GROUP], w_out.at[s], a_s.at[d], a_r.at[d], group_dev[d])
+        return remote(w_ref.at[member[d]], w_out.at[s], a_s.at[d], a_r.at[d], group_dev[d])
 
     def climb(t, j):
-        slot = (z - t) * GROUP + (g + GROUP - j) % GROUP
+        slot = (z - t) * GROUP + member[j]
         src = w_ref.at[g] if (t, j) == (0, 0) else w_out.at[slot]
         return remote(src, w_out.at[slot], up_s.at[t * GROUP + j], up_r.at[t * GROUP + j], up_dev)
 
     def sink(t, j):
-        slot = (z + t) * GROUP + (g + GROUP - j) % GROUP
+        slot = (z + t) * GROUP + member[j]
         src = w_ref.at[g] if (t, j) == (0, 0) else w_out.at[slot]
         return remote(src, w_out.at[slot], down_s.at[t * GROUP + j], down_r.at[t * GROUP + j], down_dev)
 
@@ -100,6 +101,14 @@
     own_x = pltpu.make_async_copy(n_ref, x_out.at[g], own_sem.at[1])
     block_core = remote(n_ref, x_out.at[g], core_s, core_r, core_dev)
 
+    own_m = pltpu.make_async_copy(m_ref, m_out.at[1, g], own_sem.at[2])
+
+    def spread_marks(d):
+        return remote(m_ref, m_out.at[1, g], mark_s.at[d], mark_r.at[d], group_dev[d])
+
+    marks_up = remote(m_out.at[1], m_out.at[0], mark_s.at[4], mark_r.at[4], up_dev)
+    marks_down = remote(m_out.at[1], m_out.at[2], mark_s.at[5], mark_r.at[5], down_dev)
+
     def send_z(t, j):
         @pl.when(jnp.logical_and(has_up, z - t >= 0))
         def _():
@@ -123,41 +132,63 @@
         if t + 1 <= planes - 2:
             send_z(t + 1, j)
 
+    own_m.start()
     send_z(0, 0)
-    for d in (2, 1, 3):
+    for d in (1, 2, 3):
         spread(d).start()
-    for k in range(CHUNKS):
-        over_y(k).start()
+        spread_marks(d).start()
+    over_y(0).start()
+    over_y(1).start()
     block_core.start()
     own_w.start()
     own_x.start()
-    for d in range(1, GROUP):
-        spread(d).wait_recv()
-        send_z(0, d)
 
     def take_y(k):
         over_y(k).wait_recv()
         over_x(k).start()
         over_core(k, False).start()
+        if k + 2 < CHUNKS:
+            over_y(k + 2).start()
 
     def take_x(k):
         over_x(k).wait_recv()
         over_core(k, True).start()
 
-    for k in range(CHUNKS):
-        for j in range(k * GROUP // CHUNKS, (k + 1) * GROUP // CHUNKS):
-            take_z(0, j)
-        take_y(k)
-        if k >= 1:
-            take_x(k - 1)
-        if k >= 2:
-            take_z(1, k - 2)
-    for j in range(CHUNKS - 2, GROUP):
-        take_z(1, j)
-    take_x(CHUNKS - 1)
-    for t in range(2, planes - 1):
-        for j in range(GROUP):
-            take_z(t, j)
+    def take_spread(d):
+        spread(d).wait_recv()
+        send_z(0, d)
+
+    take_spread(1)
+    take_z(0, 0)
+    take_spread(2)
+    take_spread(3)
+    take_z(0, 1)
+    own_m.wait()
+    for d in range(1, GROUP):
+        spread_marks(d).wait_recv()
+
+    @pl.when(has_up)
+    def _():
+        marks_up.start()
+
+    @pl.when(has_down)
+    def _():
+        marks_down.start()
+
+    take_z(0, 2)
+    take_y(0)
+    hops = [(0, 3)] + [(t, j) for t in range(1, planes - 1) for j in range(GROUP)]
+    moves = [(take_y, k) for k in range(1, CHUNKS)] + [(take_x, k) for k in range(CHUNKS)]
+    moves.sort(key=lambda move: move[1] + (0.5 if move[0] is take_x else -0.5))
+    done = 0
+    for i, hop in enumerate(hops):
+        take_z(*hop)
+        until = min(len(moves), (i * len(moves) + len(hops) - 1) // max(len(hops) - 1, 1))
+        for move, k in moves[done:until]:
+            move(k)
+        done = max(done, until)
+    for move, k in moves[done:]:
+        move(k)
 
     own_w.wait()
     own_x.wait()
@@ -169,6 +200,18 @@
         over_core(k, True).wait()
     for d in range(1, GROUP):
         spread(d).wait_send()
+        spread_marks(d).wait_send()
+
+    @pl.when(has_up)
+    def _():
+        marks_up.wait_send()
+        marks_down.wait_recv()
+
+    @pl.when(has_down)
+    def _():
+        marks_down.wait_send()
+        marks_up.wait_recv()
+
     for t in range(planes - 1):
         for j in range(GROUP):
 
@@ -181,7 +224,7 @@
                 sink(t, j).wait_send()
 
 
-def gather_plane(planes, normed, wcat):
+def gather_plane(planes, normed, wcat, marks):
     rows, width = normed.shape
     _, w_rows, w_cols = wcat.shape
     dma = pltpu.SemaphoreType.DMA
@@ -191,17 +234,18 @@
         out_shape=(
             jax.ShapeDtypeStruct((GROUP, rows, width), normed.dtype),
             jax.ShapeDtypeStruct((planes * GROUP, w_rows, w_cols), wcat.dtype),
+            jax.ShapeDtypeStruct((3, GROUP) + marks.shape, marks.dtype),
         ),
-        in_specs=[ANY, ANY],
-        out_specs=(ANY, ANY),
+        in_specs=[ANY, ANY, ANY],
+        out_specs=(ANY, ANY, ANY),
         scratch_shapes=[
-            dma((2,)), dma, dma, dma((CHUNKS,)), dma((CHUNKS,)), dma((CHUNKS,)), dma((CHUNKS,)),
+            dma((3,)), dma, dma, dma((CHUNKS,)), dma((CHUNKS,)), dma((CHUNKS,)), dma((CHUNKS,)),
             dma((2 * CHUNKS,)), dma((2 * CHUNKS,)), dma((GROUP,)), dma((GROUP,)),
-            dma((hops,)), dma((hops,)), dma((hops,)), dma((hops,)),
+            dma((hops,)), dma((hops,)), dma((hops,)), dma((hops,)), dma((6,)), dma((6,)),
         ],
         compiler_params=pltpu.CompilerParams(collective_id=0, has_side_effects=True),
         name="gather_plane",
-    )(normed, wcat)
+    )(normed, wcat, marks)
 
 
 def sums_kernel(part_ref, out_ref, slots, send, recv):
@@ -282,47 +326,66 @@
     )(attended)
 
 
-def attention_kernel(span_ref, q_ref, k_ref, v_ref, qm_ref, km_ref, o_ref, s_buf, m_buf, l_buf):
+def lanes(x, op):
+    out = x[:, :128]
+    for i in range(1, BLOCK // 128):
+        out = op(out, x[:, i * 128 : (i + 1) * 128])
+    return out
+
+
+def attention_kernel(span_ref, q_ref, k_ref, v_ref, qm_ref, km_ref, o_ref, s_buf):
     block = pl.program_id(0)
     first, last = span_ref[0, block], span_ref[1, block]
-    heads = q_ref.shape[1] // HEAD_DIM
+    heads = range(q_ref.shape[1] // HEAD_DIM)
+    columns = [slice(head * HEAD_DIM, (head + 1) * HEAD_DIM) for head in heads]
     rate = math.log2(math.e) / math.sqrt(HEAD_DIM)
     own = jnp.broadcast_to(qm_ref[...], (BLOCK, BLOCK))
-    for head in range(heads):
-        cols = slice(head * HEAD_DIM, (head + 1) * HEAD_DIM)
-        q = q_ref[:, cols]
-
-        def lanes(x, op):
-            out = x[:, :128]
-            for i in range(1, BLOCK // 128):
-                out = op(out, x[:, i * 128 : (i + 1) * 128])
-            return out
-
-        def score(b, highest):
-            keys = k_ref[pl.ds(pl.multiple_of(b * BLOCK, BLOCK), BLOCK), cols]
-            s = lax.dot_general(q, keys, (((1,), (1,)), ((), ())), preferred_element_type=jnp.float32)
-            s = jnp.where(own == km_ref[b], s, -1e30)
-            s_buf[b - first] = s
-            return jnp.maximum(highest, lanes(s, jnp.maximum))
-
-        highest = lax.fori_loop(first, last, score, jnp.full((BLOCK, 128), -1e30, jnp.float32))
-        m = jnp.max(highest, axis=1, keepdims=True)
-
-        def expo(b, total):
-            e = jnp.exp2((s_buf[b - first] - m) * rate)
-            s_buf[b - first] = e
-            return total + lanes(e, jnp.add)
-
-        total = lax.fori_loop(first, last, expo, jnp.zeros((BLOCK, 128), jnp.float32))
-        share = 1.0 / jnp.sum(total, axis=1, keepdims=True)
-
-        def mix(b, acc):
-            w = (s_buf[b - first] * share).astype(jnp.bfloat16)
-            values = v_ref[pl.ds(pl.multiple_of(b * BLOCK, BLOCK), BLOCK), cols]
-            return acc + jnp.dot(w, values, preferred_element_type=jnp.float32)
-
-        acc = lax.fori_loop(first, last, mix, jnp.zeros((BLOCK, HEAD_DIM), jnp.float32))
-        o_ref[:, cols] = acc.astype(o_ref.dtype)
+
+    def rows(b):
+        return pl.ds(pl.multiple_of(b * BLOCK, BLOCK), BLOCK)
+
+    def score(b, highest):
+        allowed = own == km_ref[b]
+        scores = [
+            lax.dot_general(
+                q_ref[:, columns[head]], k_ref[rows(b), columns[head]], (((1,), (1,)), ((), ())),
+                preferred_element_type=jnp.float32)
+            for head in heads
+        ]
+        out = []
+        for head in heads:
+            s = jnp.where(allowed, scores[head], -1e30)
+            s_buf[head, b - first] = s
+            out.append(jnp.maximum(highest[head], lanes(s, jnp.maximum)))
+        return tuple(out)
+
+    low = jnp.full((BLOCK, 128), -1e30, jnp.float32)
+    highest = lax.fori_loop(first, last, score, tuple(low for _ in heads))
+    tops = [jnp.max(x, axis=1, keepdims=True) for x in highest]
+
+    def expo(b, totals):
+        out = []
+        for head in heads:
+            e = jnp.exp2((s_buf[head, b - first] - tops[head]) * rate)
+            s_buf[head, b - first] = e
+            out.append(totals[head] + lanes(e, jnp.add))
+        return tuple(out)
+
+    zero = jnp.zeros((BLOCK, 128), jnp.float32)
+    totals = lax.fori_loop(first, last, expo, tuple(zero for _ in heads))
+    shares = [1.0 / jnp.sum(x, axis=1, keepdims=True) for x in totals]
+
+    def mix(b, accs):
+        out = []
+        for head in heads:
+            w = (s_buf[head, b - first] * shares[head]).astype(jnp.bfloat16)
+            out.append(accs[head] + jnp.dot(
+                w, v_ref[rows(b), columns[head]], preferred_element_type=jnp.float32))
+        return tuple(out)
+
+    accs = lax.fori_loop(first, last, mix, tuple(zero for _ in heads))
+    for head in heads:
+        o_ref[:, columns[head]] = accs[head].astype(o_ref.dtype)
 
 
 def attention(q_hat, near_k, near_v, own_marks, near_marks):
@@ -350,9 +413,7 @@
             ],
             out_specs=pl.BlockSpec((BLOCK, width), lambda i, span: (i, 0)),
             scratch_shapes=[
-                pltpu.VMEM((most, BLOCK, BLOCK), jnp.float32),
-                pltpu.VMEM((BLOCK, 128), jnp.float32),
-                pltpu.VMEM((BLOCK, 128), jnp.float32),
+                pltpu.VMEM((width // HEAD_DIM, most, BLOCK, BLOCK), jnp.float32),
             ],
         ),
         out_shape=jax.ShapeDtypeStruct((rows, width), jnp.bfloat16),
@@ -364,6 +425,31 @@
     )(span, q_hat, near_k, near_v, own_marks[:, None], near_marks.reshape(key_blocks, 1, BLOCK))
 
 
+def norm_kernel(t_ref, gain_ref, o_ref):
+    floats = t_ref[...].astype(jnp.float32)
+    square = jnp.mean(floats * floats, axis=1, keepdims=True)
+    o_ref[...] = (floats * lax.rsqrt(square + EPS) * gain_ref[...]).astype(o_ref.dtype)
+
+
+def norm_tokens(tokens, gain):
+    rows, width = tokens.shape
+    part = 128
+    return pl.pallas_call(
+        norm_kernel,
+        grid=(rows // part,),
+        in_specs=[
+            pl.BlockSpec((part, width), lambda i: (i, 0)),
+            pl.BlockSpec((1, width), lambda i: (0, 0)),
+        ],
+        out_specs=pl.BlockSpec((part, width), lambda i: (i, 0)),
+        out_shape=jax.ShapeDtypeStruct((rows, width), jnp.bfloat16),
+        compiler_params=pltpu.CompilerParams(vmem_limit_bytes=32 * 1024 * 1024),
+        cost_estimate=pl.CostEstimate(
+            flops=rows * width * 4, bytes_accessed=rows * width * 4, transcendentals=rows),
+        name="norm_tokens",
+    )(tokens, gain[None, :])
+
+
 def from_behind(shard, by):
     size = lax.axis_size("seq")
     pairs = [(i, i + by) for i in range(size) if 0 <= i + by < size]
@@ -387,11 +473,8 @@
     place = lax.axis_index("seq")
     seq = lax.axis_size("seq")
     margin = MOST - 1
-    all_marks = lax.all_gather(seg_ids, "seq", axis=0, tiled=True)
-    floats = tokens.astype(jnp.float32)
-    normed = (
-        floats * lax.rsqrt(jnp.mean(floats * floats, axis=1, keepdims=True) + EPS) * ln_gain
-    ).astype(jnp.bfloat16)
+    normed = norm_tokens(tokens, ln_gain)
+    low, high = -1, jnp.iinfo(jnp.int32).max
     if grouped:
         share = w_query.shape[1] // GROUP
         step = GROUP
@@ -399,20 +482,33 @@
         wcat = jnp.concatenate(
             [w.reshape(w.shape[0], GROUP, share) for w in (w_key, w_value, w_query)], axis=2
         ).transpose(1, 0, 2)
-        near_tokens, weights = gather_plane(seq // GROUP, normed, wcat)
+        near_tokens, weights, marks = gather_plane(
+            seq // GROUP, normed, wcat, seg_ids.reshape(-1, 128)
+        )
+        plane = place // GROUP
+        marks = marks.reshape(3, -1)
+        own_marks = marks[1]
+        left = jnp.where(plane > 0, marks[0, marks.shape[1] - margin :], low)
+        right = jnp.where(plane < seq // GROUP - 1, marks[2, :margin], high)
+        near_marks = jnp.concatenate([left, own_marks, right])
         rows = GROUP * tokens.shape[0]
         near_tokens = near_tokens.reshape(rows, tokens.shape[1])
         weights = weights.reshape(tokens.shape[1], 3 * share)
-        w_k, w_v, w_q = (weights[:, i * share : (i + 1) * share] for i in range(3))
         q_gain = lax.dynamic_slice_in_dim(q_gain, member * share, share)
         k_gain = lax.dynamic_slice_in_dim(k_gain, member * share, share)
     else:
         step = 1
         rows = tokens.shape[0]
         near_tokens = normed
-        w_k, w_v, w_q = (
-            lax.all_gather(w, "seq", axis=0, tiled=True) for w in (w_key, w_value, w_query)
+        share = w_query.shape[1]
+        weights = jnp.concatenate([w_key, w_value, w_query], axis=1)
+        weights = lax.all_gather(weights, "seq", axis=0, tiled=True)
+        all_marks = lax.all_gather(seg_ids, "seq", axis=0, tiled=True)
+        padded = jnp.concatenate(
+            [jnp.full((margin,), low, jnp.int32), all_marks, jnp.full((margin,), high, jnp.int32)]
         )
+        near_marks = lax.dynamic_slice_in_dim(padded, place * rows, rows + 2 * margin)
+        own_marks = seg_ids
 
     def project(w):
         return jnp.dot(near_tokens, w, preferred_element_type=jnp.float32)
@@ -425,16 +521,10 @@
             square = lax.psum(square, "head")
         return (part * lax.rsqrt(square[:, None] / total_channels + EPS) * gain).astype(jnp.bfloat16)
 
-    near_v = with_halo(project(w_v).astype(jnp.bfloat16), step)
-    near_k = with_halo(norm(project(w_k), k_gain), step)
-    q_hat = norm(project(w_q), q_gain)
-
-    low = jnp.full((margin,), -1, jnp.int32)
-    high = jnp.full((margin,), jnp.iinfo(jnp.int32).max, jnp.int32)
-    padded = jnp.concatenate([low, all_marks, high])
-    first = place // step * rows
-    near_marks = lax.dynamic_slice_in_dim(padded, first, rows + 2 * margin)
-    own_marks = lax.slice_in_dim(near_marks, margin, margin + rows)
+    both = project(weights[:, : 2 * share])
+    near_v = with_halo(both[:, share:].astype(jnp.bfloat16), step)
+    near_k = with_halo(norm(both[:, :share], k_gain), step)
+    q_hat = norm(project(weights[:, 2 * share :]), q_gain)
     attended = attention(q_hat, near_k, near_v, own_marks, near_marks)
     if grouped:
         attended = return_tokens(attended.reshape(GROUP, tokens.shape[0], attended.shape[1]))

time: 362 us -> 321 us (0.89)
  blocking collectives: 25.6 us -> 0 us
  local copies, waits for them, and re-layouts: 13.1 us -> 24.4 us
  Pallas kernels: 252 us -> 241 us
  other arithmetic: 20.4 us -> 11.5 us
  matrix products: 33.5 us -> 28.9 us
    all_gather x1 -> x0, blocking collectives: 25.6 us -> none  [on_device(): all_marks = lax.all_gather(seg_ids, 'seq', axis=0, tiled=True)]
    pallas_call x1, Pallas kernels: 55.8 us -> 42.3 us  [attention(): pl.pallas_call(attention_kernel, grid_spec=pltpu.PrefetchScalarGridSpec(n...]
    convert_element_type x1 -> x0, other arithmetic: 6.47 us -> none  [on_device(): normed = (floats * lax.rsqrt(jnp.mean(floats * floats, axis=1, keepdims=T...]
    unnamed x18 -> x19, local copies, waits for them, and re-layouts: 5.16 us -> 11.2 us
    dot_general x3 -> x2, matrix products: 33.5 us -> 28.9 us  [project(): return jnp.dot(near_tokens, w, preferred_element_type=jnp.float32)]
  transfers between devices with their start and end apart: 4 -> 4, of which waited for: 0 -> 0; matrix products, arithmetic and copies ran while one was open for 9% -> 8% of each run, Pallas kernels for 2% -> 2%
where the time goes in v2:
time: 321 us; the launch traced here: 319 us
  Pallas kernels  241 us (75%)
  matrix products  28.9 us (9%)
  local copies, waits for them, and re-layouts  24.4 us (8%)
  starting transfers between devices  13.3 us (4%)
  other arithmetic  11.5 us (4%)
    pallas_call x1, Pallas kernels, gather_plane(): pl.pallas_call(functools.partial(gather_kernel, planes), out_shape=(jax.S...  163 us
    pallas_call x1, Pallas kernels, attention(): pl.pallas_call(attention_kernel, grid_spec=pltpu.PrefetchScalarGridSpec(n...  42.3 us
    dot_general x2, matrix products, project(): return jnp.dot(near_tokens, w, preferred_element_type=jnp.float32)  28.9 us
    pallas_call x1, Pallas kernels, return_tokens(): pl.pallas_call(return_kernel, out_shape=jax.ShapeDtypeStruct((rows, group...  19.8 us
    ppermute x4, starting transfers between devices, from_behind(): return lax.ppermute(shard, 'seq', pairs)  13.3 us
    pallas_call x2, Pallas kernels, plane_sums(): pl.pallas_call(sums_kernel, out_shape=jax.ShapeDtypeStruct(part.shape, pa...  12.7 us
    unnamed x19, local copies, waits for them, and re-layouts  11.2 us
  transfers between devices with their start and end apart: 4, of which 0 were waited for; matrix products, arithmetic and copies ran while one was open for 8% of the time, Pallas kernels for 2%

profile of v2, /device:TPU:0, one launch (start us, length us, event | category | flops | bytes accessed | tf_op | source)
XLA Modules:
  0.0 319.3 jit_solution(3549595298778603221)
XLA Ops:
  0.0 0.7 broadcast_in_dim.16.gain_ref
  0.7 1.0 copy.26
  1.8 2.4 copy-done.1
  4.2 2.8 norm_tokens.1.n_ref
  7.0 2.2 copy-done
  9.2 1.1 maximum_bitcast_fusion.w_ref
  10.3 163.4 %gather_plane.1 = (bf16[4,768,3200]{2,1,0:T(8,128)(2,1)}, bf16[16,200,768]{2,1,0:T(8,128)(2,1)}, s32[3,4,6,128]{3,2,1,0:T(8,128)}) custom-call(bf16[768,3200]{1,0:T(8,128)(2,1)} %copy-done, bf16[4,200,768]{2,1,0:T(8,128)(2,1)} %maximum_bitcast_fusion.w_ref, s32[6,128]{1,0:T(8,128)} %bitcast.53), custom_call_target="tpu_custom_call" | custom-call | tf_op jit(solution)/shard_map/gather_plane/pallas_call | solution.py:232
  173.7 17.0 %fusion.6 = (bf16[3072,512]{1,0:T(8,128)(2,1)}, f32[3072,512]{1,0:T(8,128)S(1)}) fusion(bf16[3072,3200]{1,0:T(8,128)(2,1)} %bitcast.54, bf16[3200,768]{1,0:T(8,128)(2,1)} %bitcast.56), kind=kOutput, calls=%fused_computation.34 | convolution fusion | flops 10067902464 | bytes 32374784 | tf_op jit(solution)/shard_map/dot_general | solution.py:514
  190.8 2.7 copy-done.3
  193.4 1.1 multiply_reduce_fusion
  194.5 6.4 %plane_sums.3 = f32[24,128]{1,0:T(8,128)} custom-call(f32[24,128]{1,0:T(8,128)} %bitcast.49), custom_call_target="tpu_custom_call" | custom-call | tf_op jit(solution)/shard_map/plane_sums/pallas_call | solution.py:279
  201.6 0.8 dynamic_slice.7
  202.4 2.4 multiply_convert_fusion
  204.7 1.1 fusion.5
  205.8 1.3 collective-permute-start.1
  207.1 5.3 %collective-permute-start = (bf16[1024,256]{1,0:T(8,128)(2,1)}, bf16[1024,256]{1,0:T(8,128)(2,1)}, u32[]{:S(2)}, u32[]{:S(2)}) collective-permute-start(bf16[1024,256]{1,0:T(8,128)(2,1)} %get-tuple-element.15), channel_id=1, source_target_pairs={{0,4},{1,5},{2,6},{3,7},{4,8},{5,9},{6,10},{7,11},{8,12},{9,13},{1... | collective-permute-start | bytes 1572872 | tf_op jit(solution)/shard_map/ppermute | solution.py:456
  212.4 2.3 fusion.4
  214.8 1.3 collective-permute-start.3
  216.0 5.4 %collective-permute-start.2 = (bf16[1024,256]{1,0:T(8,128)(2,1)}, bf16[1024,256]{1,0:T(8,128)(2,1)}, u32[]{:S(2)}, u32[]{:S(2)}) collective-permute-start(bf16[1024,256]{1,0:T(8,128)(2,1)} %get-tuple-element.13), channel_id=1, source_target_pairs={{0,4},{1,5},{2,6},{3,7},{4,8},{5,9},{6,10},{7,11},{8,12},{9,13},{1... | collective-permute-start | bytes 1572872 | tf_op jit(solution)/shard_map/ppermute | solution.py:456
  221.7 11.9 %multiply_reduce_fusion.1 = (f32[3072]{0:T(1024)}, f32[3072,256]{0,1:T(8,128)}) fusion(bf16[3072,3200]{1,0:T(8,128)(2,1)} %bitcast.55, bf16[3200,768]{1,0:T(8,128)(2,1)} %bitcast.57), kind=kOutput, calls=%fused_computation.5 | convolution fusion | flops 5034734592 | bytes 24457216 | tf_op jit(solution)/shard_map/dot_general | solution.py:514
  233.6 1.2 slice.64
  234.8 1.4 broadcast_in_dim_squeeze.4.qm_ref
  236.6 3.5 %copy.18 = f32[3072,256]{1,0:T(8,128)} copy(f32[3072,256]{0,1:T(8,128)} %get-tuple-element.20) | data formatting | bytes 6291456 | tf_op jit(solution)/shard_map/dot_general | solution.py:514
  240.1 0.8 dynamic_slice.6
  240.9 6.3 %plane_sums.2 = f32[24,128]{1,0:T(8,128)} custom-call(f32[24,128]{1,0:T(8,128)} %bitcast.52), custom_call_target="tpu_custom_call" | custom-call | tf_op jit(solution)/shard_map/plane_sums/pallas_call | solution.py:279
  247.9 2.4 multiply_convert_fusion.1.q_ref
  250.4 1.5 pad_maximum_fusion.k_ref
  252.0 1.4 pad_maximum_fusion.1.v_ref
  253.4 42.3 %tile_attention.1 = bf16[3072,256]{1,0:T(8,128)(2,1)S(1)} custom-call(s32[2,12]{1,0:T(2,128)S(1)} %pad_add_fusion.1.span_ref, bf16[3072,256]{1,0:T(8,128)(2,1)S(1)} %multiply_convert_fusion.1.q_ref, bf16[5120,256]{1,0:T(8,128)(2,1)S(1)} %pad_maximum_fusion.k_ref, bf16[5120,256]{1,0:T(8,128)(2,1)S(1)} %pad_maximum_fusion.1.v_ref, ...), custom_call_target="tpu_custom_call" | custom-call | flops 3221225472 | bytes 8388608 | tf_op jit(solution)/shard_map/tile_attention/pallas_call | solution.py:402
  295.7 1.1 copy-done.2
  296.8 19.8 %return_tokens.1 = bf16[768,1024]{1,0:T(8,128)(2,1)} custom-call(bf16[4,768,256]{2,1,0:T(8,128)(2,1)} %bitcast.43), custom_call_target="tpu_custom_call" | custom-call | tf_op jit(solution)/shard_map/return_tokens/pallas_call | solution.py:318
  316.6 2.7 copy.28
  (32 shorter events, 2.2 us)
Async XLA Ops:
  1.8 2.4 copy-start.1
  4.2 5.0 %copy-start.6 = (bf16[200,1024]{1,0:T(8,128)(2,1)S(1)}, bf16[200,1024]{1,0:T(8,128)(2,1)}, u32[]{:S(2)}) copy-start(bf16[200,1024]{1,0:T(8,128)(2,1)} %param.10) | copy-start | bytes 1228804
  4.2 5.0 %copy-start.7 = (bf16[200,1024]{1,0:T(8,128)(2,1)S(1)}, bf16[200,1024]{1,0:T(8,128)(2,1)}, u32[]{:S(2)}) copy-start(bf16[200,1024]{1,0:T(8,128)(2,1)} %param.12) | copy-start | bytes 1228804
  6.9 2.2 copy-start
  190.7 2.7 copy-start.3
  204.7 16.7 %copy-start.8 = (s32[3,4,6,128]{3,2,1,0:T(8,128)S(1)}, s32[3,4,6,128]{3,2,1,0:T(8,128)}, u32[]{:S(2)}) copy-start(s32[3,4,6,128]{3,2,1,0:T(8,128)} %get-tuple-element.8) | copy-start | bytes 110596
  205.8 44.5 %collective-permute-start.1 = (bf16[1024,256]{1,0:T(8,128)(2,1)}, bf16[1024,256]{1,0:T(8,128)(2,1)}, u32[]{:S(2)}, u32[]{:S(2)}) collective-permute-start(bf16[1024,256]{1,0:T(8,128)(2,1)} %get-tuple-element.16), channel_id=1, source_target_pairs={{4,0},{5,1},{6,2},{7,3},{8,4},{9,5},{10,6},{11,7},{12,8},{13,9},{1... | collective-permute-start | bytes 1572872 | tf_op jit(solution)/shard_map/ppermute | solution.py:456
  207.1 43.2 %collective-permute-start = (bf16[1024,256]{1,0:T(8,128)(2,1)}, bf16[1024,256]{1,0:T(8,128)(2,1)}, u32[]{:S(2)}, u32[]{:S(2)}) collective-permute-start(bf16[1024,256]{1,0:T(8,128)(2,1)} %get-tuple-element.15), channel_id=1, source_target_pairs={{0,4},{1,5},{2,6},{3,7},{4,8},{5,9},{6,10},{7,11},{8,12},{9,13},{1... | collective-permute-start | bytes 1572872 | tf_op jit(solution)/shard_map/ppermute | solution.py:456
  214.8 37.1 %collective-permute-start.3 = (bf16[1024,256]{1,0:T(8,128)(2,1)}, bf16[1024,256]{1,0:T(8,128)(2,1)}, u32[]{:S(2)}, u32[]{:S(2)}) collective-permute-start(bf16[1024,256]{1,0:T(8,128)(2,1)} %get-tuple-element.14), channel_id=1, source_target_pairs={{4,0},{5,1},{6,2},{7,3},{8,4},{9,5},{10,6},{11,7},{12,8},{13,9},{1... | collective-permute-start | bytes 1572872 | tf_op jit(solution)/shard_map/ppermute | solution.py:456
  216.0 35.8 %collective-permute-start.2 = (bf16[1024,256]{1,0:T(8,128)(2,1)}, bf16[1024,256]{1,0:T(8,128)(2,1)}, u32[]{:S(2)}, u32[]{:S(2)}) collective-permute-start(bf16[1024,256]{1,0:T(8,128)(2,1)} %get-tuple-element.13), channel_id=1, source_target_pairs={{0,4},{1,5},{2,6},{3,7},{4,8},{5,9},{6,10},{7,11},{8,12},{9,13},{1... | collective-permute-start | bytes 1572872 | tf_op jit(solution)/shard_map/ppermute | solution.py:456
  221.6 11.9 %copy-start.5 = (bf16[3072,512]{1,0:T(8,128)(2,1)S(1)}, bf16[3072,512]{1,0:T(8,128)(2,1)}, u32[]{:S(2)}) copy-start(bf16[3072,512]{1,0:T(8,128)(2,1)} %get-tuple-element.21) | copy-start | bytes 9437188
  250.3 1.7 copy-start.4
  295.7 1.1 copy-start.2

commit v3 on v2

--- a/solution.py
+++ b/solution.py
@@ -14,6 +14,7 @@
 EPS = 1e-06
 GROUP = 4
 CHUNKS = 4
+PIECES = 8
 BLOCK = 256
 MESH = pl.DeviceIdType.MESH
 ANY = pl.BlockSpec(memory_space=pl.ANY)
@@ -98,10 +99,17 @@
         return remote(part, part, cf_s.at[i], cf_r.at[i], core_dev)
 
     own_w = pltpu.make_async_copy(w_ref.at[g], w_out.at[s], own_sem.at[0])
-    own_x = pltpu.make_async_copy(n_ref, x_out.at[g], own_sem.at[1])
-    block_core = remote(n_ref, x_out.at[g], core_s, core_r, core_dev)
-
-    own_m = pltpu.make_async_copy(m_ref, m_out.at[1, g], own_sem.at[2])
+    slab = rows // PIECES
+
+    def own_x(i):
+        part = pl.ds(i * slab, slab)
+        return pltpu.make_async_copy(n_ref.at[part], x_out.at[g, part], own_sem.at[2 + i])
+
+    def block_core(i):
+        part = pl.ds(i * slab, slab)
+        return remote(n_ref.at[part], x_out.at[g, part], core_s.at[i], core_r.at[i], core_dev)
+
+    own_m = pltpu.make_async_copy(m_ref, m_out.at[1, g], own_sem.at[1])
 
     def spread_marks(d):
         return remote(m_ref, m_out.at[1, g], mark_s.at[d], mark_r.at[d], group_dev[d])
@@ -139,16 +147,18 @@
         spread_marks(d).start()
     over_y(0).start()
     over_y(1).start()
-    block_core.start()
+    over_y(2).start()
     own_w.start()
-    own_x.start()
+    for i in range(PIECES):
+        block_core(i).start()
+        own_x(i).start()
 
     def take_y(k):
         over_y(k).wait_recv()
         over_x(k).start()
         over_core(k, False).start()
-        if k + 2 < CHUNKS:
-            over_y(k + 2).start()
+        if k + 3 < CHUNKS:
+            over_y(k + 3).start()
 
     def take_x(k):
         over_x(k).wait_recv()
@@ -191,8 +201,9 @@
         move(k)
 
     own_w.wait()
-    own_x.wait()
-    block_core.wait()
+    for i in range(PIECES):
+        own_x(i).wait()
+        block_core(i).wait()
     for k in range(CHUNKS):
         over_y(k).wait_send()
         over_x(k).wait_send()
@@ -236,14 +247,15 @@
             jax.ShapeDtypeStruct((planes * GROUP, w_rows, w_cols), wcat.dtype),
             jax.ShapeDtypeStruct((3, GROUP) + marks.shape, marks.dtype),
         ),
-        in_specs=[ANY, ANY, ANY],
+        in_specs=[pl.BlockSpec(memory_space=pltpu.VMEM)] * 3,
         out_specs=(ANY, ANY, ANY),
         scratch_shapes=[
-            dma((3,)), dma, dma, dma((CHUNKS,)), dma((CHUNKS,)), dma((CHUNKS,)), dma((CHUNKS,)),
+            dma((2 + PIECES,)), dma((PIECES,)), dma((PIECES,)), dma((CHUNKS,)), dma((CHUNKS,)), dma((CHUNKS,)), dma((CHUNKS,)),
             dma((2 * CHUNKS,)), dma((2 * CHUNKS,)), dma((GROUP,)), dma((GROUP,)),
             dma((hops,)), dma((hops,)), dma((hops,)), dma((hops,)), dma((6,)), dma((6,)),
         ],
-        compiler_params=pltpu.CompilerParams(collective_id=0, has_side_effects=True),
+        compiler_params=pltpu.CompilerParams(
+            collective_id=0, has_side_effects=True, vmem_limit_bytes=32 * 1024 * 1024),
         name="gather_plane",
     )(normed, wcat, marks)
 

time: 321 us -> 244 us (0.76)
  Pallas kernels: 241 us -> 165 us
    pallas_call x1, Pallas kernels: 163 us -> 90 us  [gather_plane(): pl.pallas_call(functools.partial(gather_kernel, planes), out_shape=(jax.S...]
  transfers between devices with their start and end apart: 4 -> 4, of which waited for: 0 -> 0; matrix products, arithmetic and copies ran while one was open for 8% -> 11% of each run, Pallas kernels for 2% -> 3%
where the time goes in v3:
time: 244 us; the launch traced here: 242 us
  Pallas kernels  165 us (68%)
  matrix products  30 us (12%)
  local copies, waits for them, and re-layouts  22.7 us (9%)
  starting transfers between devices  13.3 us (5%)
  other arithmetic  10.5 us (4%)
    pallas_call x1, Pallas kernels, gather_plane(): pl.pallas_call(functools.partial(gather_kernel, planes), out_shape=(jax.S...  90 us
    pallas_call x1, Pallas kernels, attention(): pl.pallas_call(attention_kernel, grid_spec=pltpu.PrefetchScalarGridSpec(n...  39.9 us
    dot_general x2, matrix products, project(): return jnp.dot(near_tokens, w, preferred_element_type=jnp.float32)  30 us
    pallas_call x1, Pallas kernels, return_tokens(): pl.pallas_call(return_kernel, out_shape=jax.ShapeDtypeStruct((rows, group...  19.8 us
    ppermute x4, starting transfers between devices, from_behind(): return lax.ppermute(shard, 'seq', pairs)  13.3 us
    pallas_call x2, Pallas kernels, plane_sums(): pl.pallas_call(sums_kernel, out_shape=jax.ShapeDtypeStruct(part.shape, pa...  12.7 us
    unnamed x19, local copies, waits for them, and re-layouts  9.58 us
  transfers between devices with their start and end apart: 4, of which 0 were waited for; matrix products, arithmetic and copies ran while one was open for 11% of the time, Pallas kernels for 3%

profile of v3, /device:TPU:0, one launch (start us, length us, event | category | flops | bytes accessed | tf_op | source)
XLA Modules:
  0.0 242.0 jit_solution(14259070939691082472)
XLA Ops:
  0.0 0.7 broadcast_in_dim.16.gain_ref
  0.7 1.0 copy.26
  1.8 2.4 copy-done
  4.2 2.8 %norm_tokens.1.n_ref = bf16[768,3200]{1,0:T(8,128)(2,1)S(1)} custom-call(bf16[768,3200]{1,0:T(8,128)(2,1)S(1)} %copy-done, f32[1,3200]{1,0:T(1,128)S(1)} %broadcast_in_dim.16.gain_ref), custom_call_target="tpu_custom_call" | custom-call | flops 9830400 | bytes 9830400 | tf_op jit(solution)/shard_map/norm_tokens/pallas_call | solution.py:449
  7.6 90.0 %gather_plane.1 = (bf16[4,768,3200]{2,1,0:T(8,128)(2,1)}, bf16[16,200,768]{2,1,0:T(8,128)(2,1)S(1)}, s32[3,4,6,128]{3,2,1,0:T(8,128)S(1)}) custom-call(bf16[768,3200]{1,0:T(8,128)(2,1)S(1)} %norm_tokens.1.n_ref, bf16[4,200,768]{2,1,0:T(8,128)(2,1)S(1)} %maximum_bitcast_fusion.w_ref, s32[6,128]{1,0:T(8,128)S(1)} %bitcast.45), custom_call_target="tpu_custom_call" | custom-call | tf_op jit(solution)/shard_map/gather_plane/pallas_call | solution.py:243
  97.7 18.1 %fusion.6 = (bf16[3072,512]{1,0:T(8,128)(2,1)}, f32[3072,512]{1,0:T(8,128)S(1)}) fusion(bf16[3072,3200]{1,0:T(8,128)(2,1)} %bitcast.56, bf16[3200,768]{1,0:T(8,128)(2,1)S(1)} %bitcast.46), kind=kOutput, calls=%fused_computation.34 | convolution fusion | flops 10067902464 | bytes 32374784 | tf_op jit(solution)/shard_map/dot_general | solution.py:526
  115.8 2.7 %copy-done.4 = f32[3072,512]{1,0:T(8,128)} copy-done((f32[3072,512]{1,0:T(8,128)}, f32[3072,512]{1,0:T(8,128)S(1)}, u32[]{:S(2)}) %copy-start.4) | copy-done | bytes 6291480
  118.5 1.1 multiply_reduce_fusion
  119.6 6.3 %plane_sums.3 = f32[24,128]{1,0:T(8,128)} custom-call(f32[24,128]{1,0:T(8,128)} %bitcast.52), custom_call_target="tpu_custom_call" | custom-call | tf_op jit(solution)/shard_map/plane_sums/pallas_call | solution.py:291
  125.9 0.7 rsqrt_bitcast_fusion
  126.6 0.8 dynamic_slice.7
  127.4 2.4 multiply_convert_fusion
  129.8 1.1 fusion.5
  130.8 1.3 collective-permute-start.1
  132.1 5.3 %collective-permute-start = (bf16[1024,256]{1,0:T(8,128)(2,1)}, bf16[1024,256]{1,0:T(8,128)(2,1)}, u32[]{:S(2)}, u32[]{:S(2)}) collective-permute-start(bf16[1024,256]{1,0:T(8,128)(2,1)} %get-tuple-element.15), channel_id=1, source_target_pairs={{0,4},{1,5},{2,6},{3,7},{4,8},{5,9},{6,10},{7,11},{8,12},{9,13},{1... | collective-permute-start | bytes 1572872 | tf_op jit(solution)/shard_map/ppermute | solution.py:468
  137.4 2.3 fusion.4
  139.8 1.3 collective-permute-start.3
  141.1 5.4 %collective-permute-start.2 = (bf16[1024,256]{1,0:T(8,128)(2,1)}, bf16[1024,256]{1,0:T(8,128)(2,1)}, u32[]{:S(2)}, u32[]{:S(2)}) collective-permute-start(bf16[1024,256]{1,0:T(8,128)(2,1)} %get-tuple-element.13), channel_id=1, source_target_pairs={{0,4},{1,5},{2,6},{3,7},{4,8},{5,9},{6,10},{7,11},{8,12},{9,13},{1... | collective-permute-start | bytes 1572872 | tf_op jit(solution)/shard_map/ppermute | solution.py:468
  146.7 11.9 %multiply_reduce_fusion.1 = (f32[3072]{0:T(1024)}, f32[3072,256]{0,1:T(8,128)}) fusion(bf16[3072,3200]{1,0:T(8,128)(2,1)} %bitcast.57, bf16[3200,768]{1,0:T(8,128)(2,1)} %bitcast.47), kind=kOutput, calls=%fused_computation.5 | convolution fusion | flops 5034734592 | bytes 24457216 | tf_op jit(solution)/shard_map/dot_general | solution.py:526
  158.6 1.2 slice.64
  159.8 1.4 broadcast_in_dim_squeeze.4.qm_ref
  161.6 3.5 %copy.18 = f32[3072,256]{1,0:T(8,128)} copy(f32[3072,256]{0,1:T(8,128)} %get-tuple-element.20) | data formatting | bytes 6291456 | tf_op jit(solution)/shard_map/dot_general | solution.py:526
  165.1 0.8 dynamic_slice.6
  165.9 6.3 %plane_sums.2 = f32[24,128]{1,0:T(8,128)} custom-call(f32[24,128]{1,0:T(8,128)} %bitcast.55), custom_call_target="tpu_custom_call" | custom-call | tf_op jit(solution)/shard_map/plane_sums/pallas_call | solution.py:291
  172.2 0.7 rsqrt_bitcast_fusion.1
  172.9 2.4 multiply_convert_fusion.1.q_ref
  175.3 1.5 pad_maximum_fusion.k_ref
  177.0 1.4 pad_maximum_fusion.1.v_ref
  178.4 39.9 %tile_attention.1 = bf16[3072,256]{1,0:T(8,128)(2,1)S(1)} custom-call(s32[2,12]{1,0:T(2,128)S(1)} %pad_add_fusion.1.span_ref, bf16[3072,256]{1,0:T(8,128)(2,1)S(1)} %multiply_convert_fusion.1.q_ref, bf16[5120,256]{1,0:T(8,128)(2,1)S(1)} %pad_maximum_fusion.k_ref, bf16[5120,256]{1,0:T(8,128)(2,1)S(1)} %pad_maximum_fusion.1.v_ref, ...), custom_call_target="tpu_custom_call" | custom-call | flops 3221225472 | bytes 8388608 | tf_op jit(solution)/shard_map/tile_attention/pallas_call | solution.py:414
  218.4 1.1 copy-done.1
  219.5 19.8 %return_tokens.1 = bf16[768,1024]{1,0:T(8,128)(2,1)} custom-call(bf16[4,768,256]{2,1,0:T(8,128)(2,1)} %bitcast.43), custom_call_target="tpu_custom_call" | custom-call | tf_op jit(solution)/shard_map/return_tokens/pallas_call | solution.py:330
  239.3 2.7 %copy.28 = bf16[768,1024]{1,0:T(8,128)(2,1)} copy(bf16[768,1024]{1,0:T(8,128)(2,1)} %return_tokens.1) | data formatting | bytes 3145728
  (32 shorter events, 1.4 us)
Async XLA Ops:
  1.8 2.4 copy-start
  4.2 2.8 %copy-start.7 = (bf16[200,1024]{1,0:T(8,128)(2,1)S(1)}, bf16[200,1024]{1,0:T(8,128)(2,1)}, u32[]{:S(2)}) copy-start(bf16[200,1024]{1,0:T(8,128)(2,1)} %param.10) | copy-start | bytes 1228804
  4.2 2.8 %copy-start.8 = (bf16[200,1024]{1,0:T(8,128)(2,1)S(1)}, bf16[200,1024]{1,0:T(8,128)(2,1)}, u32[]{:S(2)}) copy-start(bf16[200,1024]{1,0:T(8,128)(2,1)} %param.12) | copy-start | bytes 1228804
  6.9 0.7 copy-start.2
  97.7 18.1 %copy-start.3 = (bf16[16,200,768]{2,1,0:T(8,128)(2,1)}, bf16[16,200,768]{2,1,0:T(8,128)(2,1)S(1)}, u32[]{:S(2)}) copy-start(bf16[16,200,768]{2,1,0:T(8,128)(2,1)S(1)} %get-tuple-element.10) | copy-start | bytes 14745604
  115.8 2.7 %copy-start.4 = (f32[3072,512]{1,0:T(8,128)}, f32[3072,512]{1,0:T(8,128)S(1)}, u32[]{:S(2)}) copy-start(f32[3072,512]{1,0:T(8,128)S(1)} %get-tuple-element.22) | copy-start | bytes 18874372
  130.8 44.5 %collective-permute-start.1 = (bf16[1024,256]{1,0:T(8,128)(2,1)}, bf16[1024,256]{1,0:T(8,128)(2,1)}, u32[]{:S(2)}, u32[]{:S(2)}) collective-permute-start(bf16[1024,256]{1,0:T(8,128)(2,1)} %get-tuple-element.16), channel_id=1, source_target_pairs={{4,0},{5,1},{6,2},{7,3},{8,4},{9,5},{10,6},{11,7},{12,8},{13,9},{1... | collective-permute-start | bytes 1572872 | tf_op jit(solution)/shard_map/ppermute | solution.py:468
  132.1 43.2 %collective-permute-start = (bf16[1024,256]{1,0:T(8,128)(2,1)}, bf16[1024,256]{1,0:T(8,128)(2,1)}, u32[]{:S(2)}, u32[]{:S(2)}) collective-permute-start(bf16[1024,256]{1,0:T(8,128)(2,1)} %get-tuple-element.15), channel_id=1, source_target_pairs={{0,4},{1,5},{2,6},{3,7},{4,8},{5,9},{6,10},{7,11},{8,12},{9,13},{1... | collective-permute-start | bytes 1572872 | tf_op jit(solution)/shard_map/ppermute | solution.py:468
  139.8 37.1 %collective-permute-start.3 = (bf16[1024,256]{1,0:T(8,128)(2,1)}, bf16[1024,256]{1,0:T(8,128)(2,1)}, u32[]{:S(2)}, u32[]{:S(2)}) collective-permute-start(bf16[1024,256]{1,0:T(8,128)(2,1)} %get-tuple-element.14), channel_id=1, source_target_pairs={{4,0},{5,1},{6,2},{7,3},{8,4},{9,5},{10,6},{11,7},{12,8},{13,9},{1... | collective-permute-start | bytes 1572872 | tf_op jit(solution)/shard_map/ppermute | solution.py:468
  141.1 35.8 %collective-permute-start.2 = (bf16[1024,256]{1,0:T(8,128)(2,1)}, bf16[1024,256]{1,0:T(8,128)(2,1)}, u32[]{:S(2)}, u32[]{:S(2)}) collective-permute-start(bf16[1024,256]{1,0:T(8,128)(2,1)} %get-tuple-element.13), channel_id=1, source_target_pairs={{0,4},{1,5},{2,6},{3,7},{4,8},{5,9},{6,10},{7,11},{8,12},{9,13},{1... | collective-permute-start | bytes 1572872 | tf_op jit(solution)/shard_map/ppermute | solution.py:468
  146.7 11.9 %copy-start.6 = (bf16[3072,512]{1,0:T(8,128)(2,1)S(1)}, bf16[3072,512]{1,0:T(8,128)(2,1)}, u32[]{:S(2)}) copy-start(bf16[3072,512]{1,0:T(8,128)(2,1)} %get-tuple-element.21) | copy-start | bytes 9437188
  175.3 1.7 copy-start.5
  218.4 1.1 copy-start.1

commit v4 on v3

--- a/solution.py
+++ b/solution.py
@@ -330,7 +330,7 @@
     return pl.pallas_call(
         return_kernel,
         out_shape=jax.ShapeDtypeStruct((rows, group * width), attended.dtype),
-        in_specs=[ANY],
+        in_specs=[pl.BlockSpec(memory_space=pltpu.VMEM)],
         out_specs=ANY,
         scratch_shapes=[dma, dma((GROUP,)), dma((GROUP,))],
         compiler_params=pltpu.CompilerParams(collective_id=2, has_side_effects=True),
@@ -460,6 +460,33 @@
             flops=rows * width * 4, bytes_accessed=rows * width * 4, transcendentals=rows),
         name="norm_tokens",
     )(tokens, gain[None, :])
+
+
+def project_kernel(x_ref, w_ref, *o_refs):
+    part = jnp.dot(x_ref[...], w_ref[...], preferred_element_type=jnp.float32)
+    width = o_refs[0].shape[1]
+    for i, o_ref in enumerate(o_refs):
+        o_ref[...] = part[:, i * width : (i + 1) * width].astype(o_ref.dtype)
+
+
+def project(x, weights, width, place, kinds):
+    rows, depth = x.shape
+    cols = width * len(kinds)
+    return pl.pallas_call(
+        project_kernel,
+        grid=(rows // BLOCK,),
+        in_specs=[
+            pl.BlockSpec((BLOCK, depth), lambda i: (i, 0)),
+            pl.BlockSpec((depth, cols), lambda i: (0, place)),
+        ],
+        out_specs=tuple(pl.BlockSpec((BLOCK, width), lambda i: (i, 0)) for _ in kinds),
+        out_shape=tuple(jax.ShapeDtypeStruct((rows, width), kind) for kind in kinds),
+        compiler_params=pltpu.CompilerParams(vmem_limit_bytes=40 * 1024 * 1024),
+        cost_estimate=pl.CostEstimate(
+            flops=2 * rows * depth * cols, bytes_accessed=2 * depth * (rows + cols) + 4 * rows * cols,
+            transcendentals=0),
+        name="project",
+    )(x, weights)
 
 
 def from_behind(shard, by):
@@ -522,9 +549,6 @@
         near_marks = lax.dynamic_slice_in_dim(padded, place * rows, rows + 2 * margin)
         own_marks = seg_ids
 
-    def project(w):
-        return jnp.dot(near_tokens, w, preferred_element_type=jnp.float32)
-
     def norm(part, gain):
         square = jnp.sum(part * part, axis=1)
         if grouped:
@@ -533,10 +557,11 @@
             square = lax.psum(square, "head")
         return (part * lax.rsqrt(square[:, None] / total_channels + EPS) * gain).astype(jnp.bfloat16)
 
-    both = project(weights[:, : 2 * share])
-    near_v = with_halo(both[:, share:].astype(jnp.bfloat16), step)
-    near_k = with_halo(norm(both[:, :share], k_gain), step)
-    q_hat = norm(project(weights[:, 2 * share :]), q_gain)
+    key_part, v_hat = project(near_tokens, weights, share, 0, (jnp.float32, jnp.bfloat16))
+    near_v = with_halo(v_hat, step)
+    near_k = with_halo(norm(key_part, k_gain), step)
+    (queries,) = project(near_tokens, weights, share, 2, (jnp.float32,))
+    q_hat = norm(queries, q_gain)
     attended = attention(q_hat, near_k, near_v, own_marks, near_marks)
     if grouped:
         attended = return_tokens(attended.reshape(GROUP, tokens.shape[0], attended.shape[1]))

time: 244 us -> 243 us (level); the launches traced: 242 us -> 238 us
  Pallas kernels: 165 us -> 198 us
  matrix products: 30 us -> 0 us
  local copies, waits for them, and re-layouts: 22.7 us -> 19.1 us
  other arithmetic: 10.5 us -> 7.98 us
    pallas_call x0 -> x2, Pallas kernels: none -> 31.2 us  [project(): pl.pallas_call(project_kernel, grid=(rows // BLOCK,), in_specs=[pl.BlockS...]
    dot_general x2 -> x0, matrix products: 30 us -> none  [project(): return jnp.dot(near_tokens, w, preferred_element_type=jnp.float32)]
    convert_element_type x2, other arithmetic: 4.73 us -> 0.95 us  [norm(): (part * lax.rsqrt(square[:, None] / total_channels + EPS) * gain).astype(...]
    dot_general x1 -> x0, local copies, waits for them, and re-layouts: 3.52 us -> none  [project(): return jnp.dot(near_tokens, w, preferred_element_type=jnp.float32)]
    unnamed x19 -> x27, local copies, waits for them, and re-layouts: 9.58 us -> 10.7 us
  transfers between devices with their start and end apart: 4 -> 4, of which waited for: 0 -> 0; matrix products, arithmetic and copies ran while one was open for 11% -> 4% of each run, Pallas kernels for 3% -> 8%
where the time goes in v4:
time: 243 us; the launch traced here: 238 us
  Pallas kernels  198 us (81%)
  local copies, waits for them, and re-layouts  19.1 us (8%)
  starting transfers between devices  13.3 us (5%)
  other arithmetic  7.98 us (3%)
    pallas_call x1, Pallas kernels, gather_plane(): pl.pallas_call(functools.partial(gather_kernel, planes), out_shape=(jax.S...  90 us
    pallas_call x1, Pallas kernels, attention(): pl.pallas_call(attention_kernel, grid_spec=pltpu.PrefetchScalarGridSpec(n...  39.9 us
    pallas_call x2, Pallas kernels, project(): pl.pallas_call(project_kernel, grid=(rows // BLOCK,), in_specs=[pl.BlockS...  31.2 us
    pallas_call x1, Pallas kernels, return_tokens(): pl.pallas_call(return_kernel, out_shape=jax.ShapeDtypeStruct((rows, group...  21 us
    ppermute x4, starting transfers between devices, from_behind(): return lax.ppermute(shard, 'seq', pairs)  13.3 us
    pallas_call x2, Pallas kernels, plane_sums(): pl.pallas_call(sums_kernel, out_shape=jax.ShapeDtypeStruct(part.shape, pa...  12.7 us
    unnamed x27, local copies, waits for them, and re-layouts  10.7 us
  transfers between devices with their start and end apart: 4, of which 0 were waited for; matrix products, arithmetic and copies ran while one was open for 4% of the time, Pallas kernels for 8%

profile of v4, /device:TPU:0, one launch (start us, length us, event | category | flops | bytes accessed | tf_op | source)
XLA Modules:
  0.0 238.2 jit_solution(21168296279531374)
XLA Ops:
  0.0 0.7 broadcast_in_dim.16.gain_ref
  0.7 1.0 copy.23
  1.8 2.4 %copy-done = bf16[768,3200]{1,0:T(8,128)(2,1)S(1)} copy-done((bf16[768,3200]{1,0:T(8,128)(2,1)S(1)}, bf16[768,3200]{1,0:T(8,128)(2,1)}, u32[]{:S(2)}) %copy-start) | copy-done | bytes 4915224
  4.2 2.8 %norm_tokens.1.n_ref = bf16[768,3200]{1,0:T(8,128)(2,1)S(1)} custom-call(bf16[768,3200]{1,0:T(8,128)(2,1)S(1)} %copy-done, f32[1,3200]{1,0:T(1,128)S(1)} %broadcast_in_dim.16.gain_ref), custom_call_target="tpu_custom_call" | custom-call | flops 9830400 | bytes 9830400 | tf_op jit(solution)/shard_map/norm_tokens/pallas_call | solution.py:449
  7.1 0.5 copy-done.8
  7.6 90.0 %gather_plane.1 = (bf16[4,768,3200]{2,1,0:T(8,128)(2,1)}, bf16[16,200,768]{2,1,0:T(8,128)(2,1)S(1)}, s32[3,4,6,128]{3,2,1,0:T(8,128)S(1)}) custom-call(bf16[768,3200]{1,0:T(8,128)(2,1)S(1)} %norm_tokens.1.n_ref, bf16[4,200,768]{2,1,0:T(8,128)(2,1)S(1)} %maximum_bitcast_fusion.w_ref, s32[6,128]{1,0:T(8,128)S(1)} %bitcast.45), custom_call_target="tpu_custom_call" | custom-call | tf_op jit(solution)/shard_map/gather_plane/pallas_call | solution.py:243
  97.7 17.6 %project.3 = (f32[3072,256]{1,0:T(8,128)S(1)}, bf16[3072,256]{1,0:T(8,128)(2,1)S(1)}) custom-call(bf16[3072,3200]{1,0:T(8,128)(2,1)} %bitcast.46, bf16[3200,768]{1,0:T(8,128)(2,1)S(1)} %bitcast.41), custom_call_target="tpu_custom_call" | custom-call | flops 10066329600 | bytes 29229056 | tf_op jit(solution)/shard_map/project/pallas_call | solution.py:475
  115.3 1.2 copy-done.3
  116.5 1.1 multiply_reduce_fusion
  117.6 6.3 %plane_sums.3 = f32[24,128]{1,0:T(8,128)} custom-call(f32[24,128]{1,0:T(8,128)} %bitcast.52), custom_call_target="tpu_custom_call" | custom-call | tf_op jit(solution)/shard_map/plane_sums/pallas_call | solution.py:291
  123.9 0.7 rsqrt_bitcast_fusion
  124.7 0.8 dynamic_slice.7
  125.9 1.1 fusion.1
  127.0 1.3 collective-permute-start.1
  128.3 5.4 %collective-permute-start = (bf16[1024,256]{1,0:T(8,128)(2,1)}, bf16[1024,256]{1,0:T(8,128)(2,1)}, u32[]{:S(2)}, u32[]{:S(2)}) collective-permute-start(bf16[1024,256]{1,0:T(8,128)(2,1)} %get-tuple-element.19), channel_id=1, source_target_pairs={{0,4},{1,5},{2,6},{3,7},{4,8},{5,9},{6,10},{7,11},{8,12},{9,13},{1... | collective-permute-start | bytes 1572872 | tf_op jit(solution)/shard_map/ppermute | solution.py:495
  133.7 1.1 fusion
  134.8 1.3 collective-permute-start.3
  136.1 5.3 %collective-permute-start.2 = (bf16[1024,256]{1,0:T(8,128)(2,1)}, bf16[1024,256]{1,0:T(8,128)(2,1)}, u32[]{:S(2)}, u32[]{:S(2)}) collective-permute-start(bf16[1024,256]{1,0:T(8,128)(2,1)} %get-tuple-element.17), channel_id=1, source_target_pairs={{0,4},{1,5},{2,6},{3,7},{4,8},{5,9},{6,10},{7,11},{8,12},{9,13},{1... | collective-permute-start | bytes 1572872 | tf_op jit(solution)/shard_map/ppermute | solution.py:495
  141.7 2.4 %copy-done.2 = bf16[16,200,768]{2,1,0:T(8,128)(2,1)S(1)} copy-done((bf16[16,200,768]{2,1,0:T(8,128)(2,1)S(1)}, bf16[16,200,768]{2,1,0:T(8,128)(2,1)}, u32[]{:S(2)}) %copy-start.2) | copy-done | bytes 4915224
  144.1 13.6 %project.2 = f32[3072,256]{1,0:T(8,128)S(1)} custom-call(bf16[3072,3200]{1,0:T(8,128)(2,1)} %bitcast.47, bf16[3200,768]{1,0:T(8,128)(2,1)S(1)} %bitcast.42), custom_call_target="tpu_custom_call" | custom-call | flops 5033164800 | bytes 24444928 | tf_op jit(solution)/shard_map/project/pallas_call | solution.py:475
  157.7 2.6 %broadcast_in_dim_squeeze.4.qm_ref = s32[3072,1]{1,0:T(8,128)} reshape(s32[1,4,6,128]{3,2,1,0:T(8,128)S(1)} %slice.29) | data formatting | bytes 24576 | tf_op jit(solution)/shard_map/broadcast_in_dim;squeeze | solution.py:437
  160.6 0.8 dynamic_slice.6
  161.4 1.1 multiply_reduce_fusion.1
  162.5 6.3 %plane_sums.2 = f32[24,128]{1,0:T(8,128)} custom-call(f32[24,128]{1,0:T(8,128)} %bitcast.53), custom_call_target="tpu_custom_call" | custom-call | tf_op jit(solution)/shard_map/plane_sums/pallas_call | solution.py:291
  168.8 0.8 rsqrt_bitcast_fusion.1
  169.7 0.5 multiply_convert_fusion.1.q_ref
  170.2 1.5 pad_maximum_fusion.k_ref
  171.9 1.5 pad_maximum_fusion.1.v_ref
  173.5 39.9 %tile_attention.1 = bf16[3072,256]{1,0:T(8,128)(2,1)S(1)} custom-call(s32[2,12]{1,0:T(2,128)S(1)} %pad_add_fusion.1.span_ref, bf16[3072,256]{1,0:T(8,128)(2,1)S(1)} %multiply_convert_fusion.1.q_ref, bf16[5120,256]{1,0:T(8,128)(2,1)S(1)} %pad_maximum_fusion.k_ref, bf16[5120,256]{1,0:T(8,128)(2,1)S(1)} %pad_maximum_fusion.1.v_ref, s32[3072,1]{1,0:T(8,128)S(1)} %copy-done.6, ...), custom_call_target="tpu_custom_call" | custom-call | flops 3221225472 | bytes 8388608 | tf_op jit(solution)/shard_map/tile_attention/pallas_call | solution.py:414
  213.4 1.1 copy-done.7
  214.6 21.0 %return_tokens.1 = bf16[768,1024]{1,0:T(8,128)(2,1)} custom-call(bf16[4,768,256]{2,1,0:T(8,128)(2,1)} %bitcast.43), custom_call_target="tpu_custom_call" | custom-call | tf_op jit(solution)/shard_map/return_tokens/pallas_call | solution.py:330
  235.6 2.7 %copy.25 = bf16[768,1024]{1,0:T(8,128)(2,1)} copy(bf16[768,1024]{1,0:T(8,128)(2,1)} %return_tokens.1) | data formatting | bytes 3145728
  (39 shorter events, 1.5 us)
Async XLA Ops:
  1.8 2.4 %copy-start = (bf16[768,3200]{1,0:T(8,128)(2,1)S(1)}, bf16[768,3200]{1,0:T(8,128)(2,1)}, u32[]{:S(2)}) copy-start(bf16[768,3200]{1,0:T(8,128)(2,1)} %t_ref.1) | copy-start | bytes 14745604
  4.2 2.8 %copy-start.11 = (bf16[200,1024]{1,0:T(8,128)(2,1)S(1)}, bf16[200,1024]{1,0:T(8,128)(2,1)}, u32[]{:S(2)}) copy-start(bf16[200,1024]{1,0:T(8,128)(2,1)} %param.10) | copy-start | bytes 1228804
  4.2 2.8 %copy-start.12 = (bf16[200,1024]{1,0:T(8,128)(2,1)S(1)}, bf16[200,1024]{1,0:T(8,128)(2,1)}, u32[]{:S(2)}) copy-start(bf16[200,1024]{1,0:T(8,128)(2,1)} %param.12) | copy-start | bytes 1228804
  6.9 0.7 copy-start.8
  97.7 17.6 %copy-start.1 = (bf16[16,200,768]{2,1,0:T(8,128)(2,1)}, bf16[16,200,768]{2,1,0:T(8,128)(2,1)S(1)}, u32[]{:S(2)}) copy-start(bf16[16,200,768]{2,1,0:T(8,128)(2,1)S(1)} %get-tuple-element.12) | copy-start | bytes 14745604
  115.3 1.2 copy-start.3
  125.4 8.3 %copy-start.4 = (bf16[3072,256]{1,0:T(8,128)(2,1)S(1)}, bf16[3072,256]{1,0:T(8,128)(2,1)}, u32[]{:S(2)}) copy-start(bf16[3072,256]{1,0:T(8,128)(2,1)} %copy-done.3) | copy-start | bytes 4718596
  125.9 8.9 %copy-start.9 = (bf16[3072,256]{1,0:T(8,128)(2,1)}, bf16[3072,256]{1,0:T(8,128)(2,1)S(1)}, u32[]{:S(2)}) copy-start(bf16[3072,256]{1,0:T(8,128)(2,1)S(1)} %multiply_convert_fusion) | copy-start | bytes 4718596
  127.0 43.1 %collective-permute-start.1 = (bf16[1024,256]{1,0:T(8,128)(2,1)}, bf16[1024,256]{1,0:T(8,128)(2,1)}, u32[]{:S(2)}, u32[]{:S(2)}) collective-permute-start(bf16[1024,256]{1,0:T(8,128)(2,1)} %get-tuple-element.20), channel_id=1, source_target_pairs={{4,0},{5,1},{6,2},{7,3},{8,4},{9,5},{10,6},{11,7},{12,8},{13,9},{1... | collective-permute-start | bytes 1572872 | tf_op jit(solution)/shard_map/ppermute | solution.py:495
  128.3 41.8 %collective-permute-start = (bf16[1024,256]{1,0:T(8,128)(2,1)}, bf16[1024,256]{1,0:T(8,128)(2,1)}, u32[]{:S(2)}, u32[]{:S(2)}) collective-permute-start(bf16[1024,256]{1,0:T(8,128)(2,1)} %get-tuple-element.19), channel_id=1, source_target_pairs={{0,4},{1,5},{2,6},{3,7},{4,8},{5,9},{6,10},{7,11},{8,12},{9,13},{1... | collective-permute-start | bytes 1572872 | tf_op jit(solution)/shard_map/ppermute | solution.py:495
  134.8 36.9 %collective-permute-start.3 = (bf16[1024,256]{1,0:T(8,128)(2,1)}, bf16[1024,256]{1,0:T(8,128)(2,1)}, u32[]{:S(2)}, u32[]{:S(2)}) collective-permute-start(bf16[1024,256]{1,0:T(8,128)(2,1)} %get-tuple-element.18), channel_id=1, source_target_pairs={{4,0},{5,1},{6,2},{7,3},{8,4},{9,5},{10,6},{11,7},{12,8},{13,9},{1... | collective-permute-start | bytes 1572872 | tf_op jit(solution)/shard_map/ppermute | solution.py:495
  136.1 35.6 %collective-permute-start.2 = (bf16[1024,256]{1,0:T(8,128)(2,1)}, bf16[1024,256]{1,0:T(8,128)(2,1)}, u32[]{:S(2)}, u32[]{:S(2)}) collective-permute-start(bf16[1024,256]{1,0:T(8,128)(2,1)} %get-tuple-element.17), channel_id=1, source_target_pairs={{0,4},{1,5},{2,6},{3,7},{4,8},{5,9},{6,10},{7,11},{8,12},{9,13},{1... | collective-permute-start | bytes 1572872 | tf_op jit(solution)/shard_map/ppermute | solution.py:495
  141.7 2.4 %copy-start.2 = (bf16[16,200,768]{2,1,0:T(8,128)(2,1)S(1)}, bf16[16,200,768]{2,1,0:T(8,128)(2,1)}, u32[]{:S(2)}) copy-start(bf16[16,200,768]{2,1,0:T(8,128)(2,1)} %copy-done.1) | copy-start | bytes 14745604
  168.8 1.4 copy-start.10
  170.1 1.7 copy-start.5
  171.7 1.8 copy-start.6
  213.4 1.1 copy-start.7
